TPU v7x, 32 devices: a whole 2x2x4 slice. The times are simulated.
32 devices in a mesh: qrow: 4 (over x, core), qcol: 4 (over z), grp: 2 (over y).
Axes of the slice: x: 2, y: 2, z: 4, core: 2. Of those that a mesh axis runs over, the one named last changes fastest.
Arguments:
- density: float32 [512, 3, 128, 128], P(('qrow', 'qcol', 'grp')), may hold values from -1 to 1.5, as said below
- pattern: int32 [512, 3], P(('qrow', 'qcol', 'grp')), may hold values from 0 to 1, as said below
- qm_sites: float32 [4, 512], P(None, ('qrow', 'qcol', 'grp')), may hold values from 0 to 8, as said below
- positions: float32 [3, 8, 8, 4, 128], P(None, 'qrow', 'qcol', 'grp'), may hold values from 0 to 1
- atom_types: int32 [8, 8, 4, 128], P('qrow', 'qcol', 'grp'), may hold values from 0 to 7
- charges: float32 [8, 8, 4, 128], P('qrow', 'qcol', 'grp'), may hold values from -4 to 4
- eps_table: float32 [8], replicated, may hold values from 0.2 to 2
- embed_atoms: int32 [32, 32, 128], P(('qrow', 'qcol', 'grp')), may hold values from 0 to 1023
- embed_counts: int32 [32, 32], P(('qrow', 'qcol', 'grp')), may hold values from 0 to 128, as said below
Outputs:
- purified: float32 [512, 3, 128, 128], P(('qrow', 'qcol', 'grp'))
- mm_force: float32 [3, 8, 8, 4, 128], P(None, 'qrow', 'qcol', 'grp')
Inputs may be any that keep to these rules, and one draw needn't show every extreme that they name: `pattern`: column 1 is 1 in every block row; column 0 is 1 in every block row i with i mod 16 < 1, and column 2 in every block row i with i mod 16 >= 15. `density`: dominant diagonal near 0.5 with small entries elsewhere. `qm_sites`: centres lie in the MM box; the fourth row lies in 0.2 to 0.8. `embed_counts`: one owner, drawn from the seed, receives 128 atoms from every device.
All inputs are finite; a program needn't handle non-finite values.
Results may differ from a plain program's by a relative error of at most 0.0003.
Values sent between devices are 32-bit elements; how exact they have to be, the bound alone decides.
A program may use at most 128 MiB of HBM per device.

v0:
```python
import jax
import jax.numpy as jnp
from jax import lax
from jax.sharding import PartitionSpec as P

W = 1
ITERS = 6


SIGMA_SQ = 0.25
EMBED = 20.0
SOFTEN = 1.0


def passed_along(value, axis, by):
    devices = lax.axis_size(axis)
    pairs = [(i, i + by) for i in range(devices) if 0 <= i + by < devices]
    return lax.ppermute(value, axis, pairs)


def padded(cells, sides, width):
    for axis, dim in sides:
        count = lax.axis_size(axis)
        head = lax.slice_in_dim(cells, 0, width, axis=dim)
        tail = lax.slice_in_dim(cells, cells.shape[dim] - width, cells.shape[dim], axis=dim)
        cells = jnp.concatenate(
            [
                lax.ppermute(tail, axis, [(i, (i + 1) % count) for i in range(count)]),
                cells,
                lax.ppermute(head, axis, [((i + 1) % count, i) for i in range(count)]),
            ],
            axis=dim,
        )
    return cells


def keep_of(pattern, first_row, total_rows):
    row_ids = first_row + jnp.arange(pattern.shape[0], dtype=jnp.int32)[:, None]
    column_ids = row_ids + jnp.arange(pattern.shape[1], dtype=jnp.int32)[None, :] - W
    inside = (column_ids >= 0) & (column_ids < total_rows) & (pattern > 0)
    return jnp.where(inside, 1.0, 0.0).astype(jnp.float32)


def band_product(left_band, extended, keep_mask):
    row_count = left_band.shape[0]
    width_band = left_band.shape[1]
    half_band = (width_band - 1) // 2
    results = []
    for target in range(width_band):
        total = None
        for window_row in range(width_band):
            offset = target - window_row + half_band
            if 0 <= offset < width_band:
                term = jnp.einsum(
                    "rpk,rkq->rpq",
                    left_band[:, window_row],
                    extended[window_row : window_row + row_count, offset],
                    precision=lax.Precision.HIGHEST,
                )
                total = term if total is None else total + term
        results.append(total)
    return jnp.stack(results, axis=1) * keep_mask[:, :, None, None]


def with_neighbours(current):
    from_below = passed_along(current[-W:], ("qrow", "qcol", "grp"), 1)
    from_above = passed_along(current[:W], ("qrow", "qcol", "grp"), -1)
    return jnp.concatenate([from_below, current, from_above], axis=0)


def pair_force(own_cells, neighbour, offsets):
    delta_list = [
        own_cells[axis_id][..., :, None] - neighbour[axis_id][..., None, :] - offsets[axis_id]
        for axis_id in range(3)
    ]
    distance_sq = (
        delta_list[0] * delta_list[0]
        + delta_list[1] * delta_list[1]
        + delta_list[2] * delta_list[2]
    )
    weight_pair = (
        own_cells[3][..., :, None] * neighbour[3][..., None, :] * jnp.exp(-distance_sq / SIGMA_SQ)
    )
    return jnp.stack(
        [jnp.sum(weight_pair * component, axis=-1) for component in delta_list], axis=0
    )


def embed_term(coords, charge_row, centers, block_charge):
    gap_list = [coords[axis_id][:, None, :] - centers[axis_id][:, :, None] for axis_id in range(3)]
    total_sq = (
        gap_list[0] * gap_list[0] + gap_list[1] * gap_list[1] + gap_list[2] * gap_list[2] + SOFTEN
    )
    factor = block_charge[:, :, None] / (total_sq * jnp.sqrt(total_sq))
    return jnp.stack(
        [EMBED * charge_row * jnp.sum(factor * gap_part, axis=1) for gap_part in gap_list], axis=0
    )


def send_rows(outgoing):
    return lax.all_to_all(
        outgoing, ("qrow", "qcol", "grp"), split_axis=1, concat_axis=1, tiled=True
    )


def return_rows(force_rows):
    return lax.all_to_all(
        force_rows, ("qrow", "qcol", "grp"), split_axis=1, concat_axis=1, tiled=True
    )


def per_device(
    density, pattern, qm_sites, positions, atom_types, charges, eps_table, embed_atoms, embed_counts
):
    row_count = density.shape[0]
    device_count = lax.axis_size("qrow") * lax.axis_size("qcol") * lax.axis_size("grp")
    first_row = lax.axis_index(("qrow", "qcol", "grp")) * row_count
    keep_mask = keep_of(pattern, first_row, row_count * device_count)
    grid_shape = positions.shape[1:]
    atom_count = grid_shape[0] * grid_shape[1] * grid_shape[2] * grid_shape[3]
    anchor = [
        lax.axis_index("qrow") * grid_shape[0],
        lax.axis_index("qcol") * grid_shape[1],
        lax.axis_index("grp") * grid_shape[2],
    ]
    coords = jnp.stack(
        [
            positions[axis_id]
            + (lax.broadcasted_iota(jnp.int32, grid_shape, axis_id) + anchor[axis_id]).astype(
                jnp.float32
            )
            for axis_id in range(3)
        ],
        axis=0,
    )
    payload = jnp.concatenate([coords, charges[None]], axis=0).reshape(4, atom_count)
    atom_list = embed_atoms[0]
    count_list = embed_counts[0]
    chosen = jnp.take(payload, atom_list, axis=1)
    live = jnp.arange(atom_list.shape[1], dtype=jnp.int32)[None, :] < count_list[:, None]
    outgoing = jnp.concatenate([chosen[:3], jnp.where(live, chosen[3], 0.0)[None]], axis=0)
    received = send_rows(outgoing)
    type_ids = jnp.arange(eps_table.shape[0], dtype=jnp.int32)[:, None, None, None, None]
    strength = jnp.sqrt(
        jnp.sum(
            jnp.where(atom_types[None] == type_ids, eps_table[:, None, None, None, None], 0.0),
            axis=0,
        )
    )
    stacked = jnp.concatenate([positions, strength[None]], axis=0)
    extended_cells = padded(stacked, (("qrow", 1), ("qcol", 2), ("grp", 3)), 1)
    cells_x, cells_y, cells_z = (grid_shape[0], grid_shape[1], grid_shape[2])
    force_total = jnp.zeros_like(positions)
    for shift_x in (-1, 0, 1):
        for shift_y in (-1, 0, 1):
            for shift_z in (-1, 0, 1):
                neighbour = extended_cells[
                    :,
                    1 + shift_x : 1 + shift_x + cells_x,
                    1 + shift_y : 1 + shift_y + cells_y,
                    1 + shift_z : 1 + shift_z + cells_z,
                ]
                force_total = force_total + pair_force(
                    stacked, neighbour, (shift_x, shift_y, shift_z)
                )
    current = density * keep_mask[:, :, None, None]
    for sweep_index in range(ITERS):
        extended = with_neighbours(current)
        square = band_product(current, extended, keep_mask)
        cube_term = band_product(square, extended, keep_mask)
        current = 3.0 * square - 2.0 * cube_term
    diag_mean = jnp.mean(jnp.diagonal(current[:, W], axis1=1, axis2=2), axis=1)
    qm_charge = qm_sites[3] - diag_mean
    owner_force = embed_term(
        received[:3], received[3], qm_sites[:3][:, None, :], qm_charge[None, :]
    )
    returned = return_rows(owner_force)
    empty = jnp.zeros((3, atom_count), jnp.float32)
    embed_force = (
        empty.at[:, atom_list.reshape(-1)].add(returned.reshape(3, -1)).reshape((3,) + grid_shape)
    )
    return (current, force_total + embed_force)


def solution(mesh):
    in_specs = (
        P(("qrow", "qcol", "grp"), None, None, None),
        P(("qrow", "qcol", "grp"), None),
        P(None, ("qrow", "qcol", "grp")),
        P(None, "qrow", "qcol", "grp", None),
        P("qrow", "qcol", "grp", None),
        P("qrow", "qcol", "grp", None),
        P(),
        P(("qrow", "qcol", "grp"), None, None),
        P(("qrow", "qcol", "grp"), None),
    )
    out_specs = (P(("qrow", "qcol", "grp"), None, None, None), P(None, "qrow", "qcol", "grp", None))
    return jax.shard_map(
        per_device, mesh=mesh, in_specs=in_specs, out_specs=out_specs, check_vma=False
    )
```

profile of v0, /device:TPU:0, one launch (start us, length us, event | category | flops | bytes accessed | tf_op | source)
XLA Modules:
  0.0 305.3 jit_solution(7845693902758093669)
XLA Ops:
  4.3 5.5 %collective-permute-start = (f32[1,3,128,128]{3,2,0,1:T(8,128)}, f32[1,3,128,128]{3,2,0,1:T(8,128)}, u32[]{:S(2)}, u32[]{:S(2)}) collective-permute-start(f32[1,3,128,128]{3,2,0,1:T(8,128)} %get-tuple-element.193), channel_id=1, source_target_pairs={{0,1},{1,2},{2,3},{3,4},{4,5},{5,6},{6,7},{7,8},{8,9},{9,10},{10,1... | collective-permute-start | bytes 589832 | tf_op jit(solution)/shard_map/ppermute | solution.py:18
  11.3 4.3 %collective-permute-start.13 = (f32[4,1,2,2,128]{4,3,2,1,0:T(2,128)S(1)}, f32[4,1,2,2,128]{4,3,2,1,0:T(2,128)S(1)}, u32[]{:S(2)}, u32[]{:S(2)}) collective-permute-start(f32[4,1,2,2,128]{4,3,2,1,0:T(2,128)S(1)} %get-tuple-element.311), channel_id=1, source_target_pairs={{8,0},{16,8},{24,16},{0,24},{9,1},{17,9},{25,17},{1,25},{10,2},{18... | collective-permute-start | bytes 24584 | tf_op jit(solution)/shard_map/ppermute | solution.py:30
  24.4 15.2 %gather_fusion = f32[4096,4]{1,0:T(8,128)} fusion(f32[4,1024]{0,1:T(8,128)} %copy.49, s32[4096]{0:T(1024)S(1)} %fusion.267), kind=kCustom, calls=%fused_computation | custom fusion | bytes 147456 | tf_op jit(solution)/shard_map/jit(_take)/gather | solution.py:139
  42.7 3.4 %all-to-all-start = ((f32[4,32,128]{2,0,1:T(4,128)}), f32[4,32,128]{2,0,1:T(4,128)S(1)}, u32[]{:S(2)}, u32[]{:S(2)}) async-start(f32[4,32,128]{2,0,1:T(4,128)} %pad_maximum_fusion.14), calls=%async_computation | async-start | bytes 131072 | tf_op jit(solution)/shard_map/all_to_all | solution.py:101
  46.1 3.7 %collective-permute-start.15 = (f32[4,4,1,2,128]{4,3,2,1,0:T(2,128)S(1)}, f32[4,4,1,2,128]{4,3,2,1,0:T(2,128)S(1)}, u32[]{:S(2)}, u32[]{:S(2)}) collective-permute-start(f32[4,4,1,2,128]{4,3,2,1,0:T(2,128)S(1)} %get-tuple-element.302), channel_id=1, source_target_pairs={{2,0},{4,2},{6,4},{0,6},{3,1},{5,3},{7,5},{1,7},{10,8},{12,10},{14... | collective-permute-start | bytes 49160 | tf_op jit(solution)/shard_map/ppermute | solution.py:30
  51.2 4.2 %collective-permute-done.14 = f32[4,4,1,2,128]{4,3,2,1,0:T(2,128)S(1)} collective-permute-done((f32[4,4,1,2,128]{4,3,2,1,0:T(2,128)S(1)}, f32[4,4,1,2,128]{4,3,2,1,0:T(2,128)S(1)}, u32[]{:S(2)}, u32[]{:S(2)}) %collective-permute-start.14) | collective-permute-done | bytes 16416 | tf_op jit(solution)/shard_map/ppermute | solution.py:28
  67.8 3.7 %multiply_reduce_fusion.40 = (f32[2,2,2,128]{3,2,1,0:T(2,128)}, f32[2,2,2,128]{3,2,1,0:T(2,128)}, f32[2,2,2,128]{3,2,1,0:T(2,128)}, f32[2,2,2,128]{3,2,1,0:T(2,1...) fusion(f32[2,2,2,128]{3,2,1,0:T(2,128)S(1)} %get-tuple-element., ...), kind=kLoop, calls=%fused_computation.507 | loop fusion | flops 7855104 | bytes 102400 | tf_op jit(solution)/shard_map/reduce_sum | solution.py:85
  71.6 3.0 multiply_reduce_fusion.37
  74.6 3.5 %multiply_reduce_fusion.53 = (f32[2,2,2,128]{3,2,1,0:T(2,128)}, f32[2,2,2,128]{3,2,1,0:T(2,128)}, f32[2,2,2,128]{3,2,1,0:T(2,128)}, f32[2,2,2,128]{3,2,1,0:T(2,1...) fusion(f32[2,2,2,128]{3,2,1,0:T(2,128)S(1)} %get-tuple-element., ...), kind=kLoop, calls=%fused_computation.535 | loop fusion | flops 10211328 | bytes 114688 | tf_op jit(solution)/shard_map/reduce_sum | solution.py:85
  78.1 3.1 %multiply_reduce_fusion.50 = (f32[2,2,2,128]{3,2,1,0:T(2,128)}, f32[2,2,2,128]{3,2,1,0:T(2,128)}, f32[2,2,2,128]{3,2,1,0:T(2,128)}, f32[2,2,2,128]{3,2,1,0:T(2,1...) fusion(f32[2,2,2,128]{3,2,1,0:T(2,128)S(1)} %get-tuple-element., ...), kind=kLoop, calls=%fused_computation.530 | loop fusion | flops 7724032 | bytes 102400 | tf_op jit(solution)/shard_map/reduce_sum | solution.py:85
  81.2 3.1 %multiply_reduce_fusion.48 = (f32[2,2,2,128]{3,2,1,0:T(2,128)}, f32[2,2,2,128]{3,2,1,0:T(2,128)}, f32[2,2,2,128]{3,2,1,0:T(2,128)}, f32[2,2,2,128]{3,2,1,0:T(2,1...) fusion(f32[2,2,2,128]{3,2,1,0:T(2,128)S(1)} %get-tuple-element., ...), kind=kLoop, calls=%fused_computation.524 | loop fusion | flops 7855104 | bytes 102400 | tf_op jit(solution)/shard_map/reduce_sum | solution.py:85
  84.3 3.4 %multiply_reduce_fusion.45 = (f32[2,2,2,128]{3,2,1,0:T(2,128)}, f32[2,2,2,128]{3,2,1,0:T(2,128)}, f32[2,2,2,128]{3,2,1,0:T(2,128)}, f32[2,2,2,128]{3,2,1,0:T(2,1...) fusion(f32[2,2,2,128]{3,2,1,0:T(2,128)S(1)} %get-tuple-element., ...), kind=kLoop, calls=%fused_computation.519 | loop fusion | flops 7724032 | bytes 102400 | tf_op jit(solution)/shard_map/reduce_sum | solution.py:85
  111.4 4.2 %collective-permute-done.2 = f32[1,3,128,128]{3,2,0,1:T(8,128)S(1)} collective-permute-done((f32[1,3,128,128]{3,2,0,1:T(8,128)S(1)}, f32[1,3,128,128]{3,2,0,1:T(8,128)S(1)}, u32[]{:S(2)}, u32[]{:S(2)}) %collective-permute-start.2) | collective-permute-done | bytes 196640 | tf_op jit(solution)/shard_map/ppermute | solution.py:18
  134.8 3.1 %collective-permute-start.4 = (f32[1,3,128,128]{3,2,0,1:T(8,128)S(1)}, f32[1,3,128,128]{3,2,0,1:T(8,128)S(1)}, u32[]{:S(2)}, u32[]{:S(2)}) collective-permute-start(f32[1,3,128,128]{3,2,0,1:T(8,128)S(1)} %get-tuple-element.185), channel_id=1, source_target_pairs={{0,1},{1,2},{2,3},{3,4},{4,5},{5,6},{6,7},{7,8},{8,9},{9,10},{10,1... | collective-permute-start | bytes 589832 | tf_op jit(solution)/shard_map/ppermute | solution.py:18
  140.4 4.9 %collective-permute-done.4 = f32[1,3,128,128]{3,2,0,1:T(8,128)S(1)} collective-permute-done((f32[1,3,128,128]{3,2,0,1:T(8,128)S(1)}, f32[1,3,128,128]{3,2,0,1:T(8,128)S(1)}, u32[]{:S(2)}, u32[]{:S(2)}) %collective-permute-start.4) | collective-permute-done | bytes 196640 | tf_op jit(solution)/shard_map/ppermute | solution.py:18
  163.7 3.8 %collective-permute-start.6 = (f32[1,3,128,128]{3,2,0,1:T(8,128)S(1)}, f32[1,3,128,128]{3,2,0,1:T(8,128)S(1)}, u32[]{:S(2)}, u32[]{:S(2)}) collective-permute-start(f32[1,3,128,128]{3,2,0,1:T(8,128)S(1)} %get-tuple-element.181), channel_id=1, source_target_pairs={{0,1},{1,2},{2,3},{3,4},{4,5},{5,6},{6,7},{7,8},{8,9},{9,10},{10,1... | collective-permute-start | bytes 589832 | tf_op jit(solution)/shard_map/ppermute | solution.py:18
  170.6 6.3 %collective-permute-done.7 = f32[1,3,128,128]{3,2,0,1:T(8,128)S(1)} collective-permute-done((f32[1,3,128,128]{3,2,0,1:T(8,128)S(1)}, f32[1,3,128,128]{3,2,0,1:T(8,128)S(1)}, u32[]{:S(2)}, u32[]{:S(2)}) %collective-permute-start.7) | collective-permute-done | bytes 196640 | tf_op jit(solution)/shard_map/ppermute | solution.py:18
  194.9 3.0 collective-permute-start.8
  201.3 7.6 %collective-permute-done.9 = f32[1,3,128,128]{3,2,0,1:T(8,128)S(1)} collective-permute-done((f32[1,3,128,128]{3,2,0,1:T(8,128)S(1)}, f32[1,3,128,128]{3,2,0,1:T(8,128)S(1)}, u32[]{:S(2)}, u32[]{:S(2)}) %collective-permute-start.9) | collective-permute-done | bytes 196640 | tf_op jit(solution)/shard_map/ppermute | solution.py:18
  233.1 7.6 %collective-permute-done.11 = f32[1,3,128,128]{3,2,0,1:T(8,128)S(1)} collective-permute-done((f32[1,3,128,128]{3,2,0,1:T(8,128)S(1)}, f32[1,3,128,128]{3,2,0,1:T(8,128)S(1)}, u32[]{:S(2)}, u32[]{:S(2)}) %collective-permute-start.11) | collective-permute-done | bytes 196640 | tf_op jit(solution)/shard_map/ppermute | solution.py:18
  257.2 6.0 %copy.52 = f32[16,128,128]{0,2,1:T(8,128)} copy(f32[16,128,128]{2,1,0:T(8,128)} %slice_bitcast_fusion) | data formatting | bytes 2097152 | tf_op jit(solution)/shard_map/squeeze | solution.py:172
  266.8 5.5 %all-to-all-start.1 = ((f32[3,32,128]{2,0,1:T(4,128)}), f32[3,32,128]{2,0,1:T(4,128)S(1)}, u32[]{:S(2)}, u32[]{:S(2)}) async-start(f32[3,32,128]{2,0,1:T(4,128)} %copy.56), calls=%async_computation.1 | async-start | bytes 131072 | tf_op jit(solution)/shard_map/all_to_all | solution.py:107
  276.5 3.2 %all-to-all-done.1 = f32[3,32,128]{2,0,1:T(4,128)S(1)} async-done(((f32[3,32,128]{2,0,1:T(4,128)}), f32[3,32,128]{2,0,1:T(4,128)S(1)}, u32[]{:S(2)}, u32[]{:S(2)}) %all-to-all-start.1) | async-done | bytes 49184 | tf_op jit(solution)/shard_map/all_to_all | solution.py:107
  280.3 22.5 %scatter_custom_fusion = f32[3,1024]{0,1:T(8,128)S(1)} fusion(s32[4096]{0:T(1024)S(1)} %bitcast.710, f32[4096,3]{1,0:T(8,128)S(1)} %copy.57, f32[]{:T(128)} %constant.137.clone.1), kind=kCustom, calls=%fused_computation.554 | custom fusion | flops 12288 | bytes 12292 | tf_op jit(solution)/shard_map/scatter-add | solution.py:180
  (320 shorter events, 168.6 us)
Async XLA Ops:
  4.3 83.5 %collective-permute-start = (f32[1,3,128,128]{3,2,0,1:T(8,128)}, f32[1,3,128,128]{3,2,0,1:T(8,128)}, u32[]{:S(2)}, u32[]{:S(2)}) collective-permute-start(f32[1,3,128,128]{3,2,0,1:T(8,128)} %get-tuple-element.193), channel_id=1, source_target_pairs={{0,1},{1,2},{2,3},{3,4},{4,5},{5,6},{6,7},{7,8},{8,9},{9,10},{10,1... | collective-permute-start | bytes 589832 | tf_op jit(solution)/shard_map/ppermute | solution.py:18
  9.8 78.0 %collective-permute-start.1 = (f32[1,3,128,128]{3,2,0,1:T(8,128)S(1)}, f32[1,3,128,128]{3,2,0,1:T(8,128)}, u32[]{:S(2)}, u32[]{:S(2)}) collective-permute-start(f32[1,3,128,128]{3,2,0,1:T(8,128)S(1)} %get-tuple-element.194), channel_id=1, source_target_pairs={{1,0},{2,1},{3,2},{4,3},{5,4},{6,5},{7,6},{8,7},{9,8},{10,9},{11,1... | collective-permute-start | bytes 589832 | tf_op jit(solution)/shard_map/ppermute | solution.py:18
  11.2 73.1 %copy-start.49 = (f32[2,2,2,128]{3,2,1,0:T(2,128)}, f32[2,2,2,128]{3,2,1,0:T(2,128)S(1)}, u32[]{:S(2)}) copy-start(f32[2,2,2,128]{3,2,1,0:T(2,128)S(1)} %get-tuple-element.322) | copy-start | bytes 12292
  11.3 11.5 %collective-permute-start.13 = (f32[4,1,2,2,128]{4,3,2,1,0:T(2,128)S(1)}, f32[4,1,2,2,128]{4,3,2,1,0:T(2,128)S(1)}, u32[]{:S(2)}, u32[]{:S(2)}) collective-permute-start(f32[4,1,2,2,128]{4,3,2,1,0:T(2,128)S(1)} %get-tuple-element.311), channel_id=1, source_target_pairs={{8,0},{16,8},{24,16},{0,24},{9,1},{17,9},{25,17},{1,25},{10,2},{18... | collective-permute-start | bytes 24584 | tf_op jit(solution)/shard_map/ppermute | solution.py:30
  15.5 30.5 %collective-permute-start.12 = (f32[4,1,2,2,128]{4,3,2,1,0:T(2,128)S(1)}, f32[4,1,2,2,128]{4,3,2,1,0:T(2,128)S(1)}, u32[]{:S(2)}, u32[]{:S(2)}) collective-permute-start(f32[4,1,2,2,128]{4,3,2,1,0:T(2,128)S(1)} %get-tuple-element.312), channel_id=1, source_target_pairs={{0,8},{8,16},{16,24},{24,0},{1,9},{9,17},{17,25},{25,1},{2,10},{10... | collective-permute-start | bytes 24584 | tf_op jit(solution)/shard_map/ppermute | solution.py:28
  23.4 60.9 %copy-start.51 = (f32[2,2,2,128]{3,2,1,0:T(2,128)}, f32[2,2,2,128]{3,2,1,0:T(2,128)S(1)}, u32[]{:S(2)}) copy-start(f32[2,2,2,128]{3,2,1,0:T(2,128)S(1)} %get-tuple-element.319) | copy-start | bytes 12292
  42.7 45.0 %all-to-all-start = ((f32[4,32,128]{2,0,1:T(4,128)}), f32[4,32,128]{2,0,1:T(4,128)S(1)}, u32[]{:S(2)}, u32[]{:S(2)}) async-start(f32[4,32,128]{2,0,1:T(4,128)} %pad_maximum_fusion.14), calls=%async_computation | async-start | bytes 131072 | tf_op jit(solution)/shard_map/all_to_all | solution.py:101
  46.1 5.1 %collective-permute-start.15 = (f32[4,4,1,2,128]{4,3,2,1,0:T(2,128)S(1)}, f32[4,4,1,2,128]{4,3,2,1,0:T(2,128)S(1)}, u32[]{:S(2)}, u32[]{:S(2)}) collective-permute-start(f32[4,4,1,2,128]{4,3,2,1,0:T(2,128)S(1)} %get-tuple-element.302), channel_id=1, source_target_pairs={{2,0},{4,2},{6,4},{0,6},{3,1},{5,3},{7,5},{1,7},{10,8},{12,10},{14... | collective-permute-start | bytes 49160 | tf_op jit(solution)/shard_map/ppermute | solution.py:30
  49.8 5.7 %collective-permute-start.14 = (f32[4,4,1,2,128]{4,3,2,1,0:T(2,128)S(1)}, f32[4,4,1,2,128]{4,3,2,1,0:T(2,128)S(1)}, u32[]{:S(2)}, u32[]{:S(2)}) collective-permute-start(f32[4,4,1,2,128]{4,3,2,1,0:T(2,128)S(1)} %get-tuple-element.301), channel_id=1, source_target_pairs={{0,2},{2,4},{4,6},{6,0},{1,3},{3,5},{5,7},{7,1},{8,10},{10,12},{12... | collective-permute-start | bytes 49160 | tf_op jit(solution)/shard_map/ppermute | solution.py:28
  50.0 34.3 %copy-start.45 = (f32[2,2,2,128]{3,2,1,0:T(2,128)}, f32[2,2,2,128]{3,2,1,0:T(2,128)S(1)}, u32[]{:S(2)}) copy-start(f32[2,2,2,128]{3,2,1,0:T(2,128)S(1)} %get-tuple-element.320) | copy-start | bytes 12292
  50.0 34.3 %copy-start.47 = (f32[2,2,2,128]{3,2,1,0:T(2,128)}, f32[2,2,2,128]{3,2,1,0:T(2,128)S(1)}, u32[]{:S(2)}) copy-start(f32[2,2,2,128]{3,2,1,0:T(2,128)S(1)} %get-tuple-element.321) | copy-start | bytes 12292
  55.6 4.0 %collective-permute-start.16 = (f32[4,4,4,1,128]{4,3,2,1,0:T(1,128)S(1)}, f32[4,4,4,1,128]{4,3,2,1,0:T(1,128)S(1)}, u32[]{:S(2)}, u32[]{:S(2)}) collective-permute-start(f32[4,4,4,1,128]{4,3,2,1,0:T(1,128)S(1)} %get-tuple-element.269), channel_id=1, source_target_pairs={{0,1},{1,0},{2,3},{3,2},{4,5},{5,4},{6,7},{7,6},{8,9},{9,8},{10,11... | collective-permute-start | bytes 98312 | tf_op jit(solution)/shard_map/ppermute | solution.py:28
  57.1 3.9 %collective-permute-start.17 = (f32[4,4,4,1,128]{4,3,2,1,0:T(1,128)S(1)}, f32[4,4,4,1,128]{4,3,2,1,0:T(1,128)S(1)}, u32[]{:S(2)}, u32[]{:S(2)}) collective-permute-start(f32[4,4,4,1,128]{4,3,2,1,0:T(1,128)S(1)} %get-tuple-element.270), channel_id=1, source_target_pairs={{1,0},{0,1},{3,2},{2,3},{5,4},{4,5},{7,6},{6,7},{9,8},{8,9},{11,10... | collective-permute-start | bytes 98312 | tf_op jit(solution)/shard_map/ppermute | solution.py:30
  106.5 9.1 %collective-permute-start.2 = (f32[1,3,128,128]{3,2,0,1:T(8,128)S(1)}, f32[1,3,128,128]{3,2,0,1:T(8,128)S(1)}, u32[]{:S(2)}, u32[]{:S(2)}) collective-permute-start(f32[1,3,128,128]{3,2,0,1:T(8,128)S(1)} %get-tuple-element.189), channel_id=1, source_target_pairs={{0,1},{1,2},{2,3},{3,4},{4,5},{5,6},{6,7},{7,8},{8,9},{9,10},{10,1... | collective-permute-start | bytes 589832 | tf_op jit(solution)/shard_map/ppermute | solution.py:18
  108.9 7.9 %collective-permute-start.3 = (f32[1,3,128,128]{3,2,0,1:T(8,128)S(1)}, f32[1,3,128,128]{3,2,0,1:T(8,128)S(1)}, u32[]{:S(2)}, u32[]{:S(2)}) collective-permute-start(f32[1,3,128,128]{3,2,0,1:T(8,128)S(1)} %get-tuple-element.190), channel_id=1, source_target_pairs={{1,0},{2,1},{3,2},{4,3},{5,4},{6,5},{7,6},{8,7},{9,8},{10,9},{11,1... | collective-permute-start | bytes 589832 | tf_op jit(solution)/shard_map/ppermute | solution.py:18
  134.8 10.5 %collective-permute-start.4 = (f32[1,3,128,128]{3,2,0,1:T(8,128)S(1)}, f32[1,3,128,128]{3,2,0,1:T(8,128)S(1)}, u32[]{:S(2)}, u32[]{:S(2)}) collective-permute-start(f32[1,3,128,128]{3,2,0,1:T(8,128)S(1)} %get-tuple-element.185), channel_id=1, source_target_pairs={{0,1},{1,2},{2,3},{3,4},{4,5},{5,6},{6,7},{7,8},{8,9},{9,10},{10,1... | collective-permute-start | bytes 589832 | tf_op jit(solution)/shard_map/ppermute | solution.py:18
  137.9 8.0 %collective-permute-start.5 = (f32[1,3,128,128]{3,2,0,1:T(8,128)S(1)}, f32[1,3,128,128]{3,2,0,1:T(8,128)S(1)}, u32[]{:S(2)}, u32[]{:S(2)}) collective-permute-start(f32[1,3,128,128]{3,2,0,1:T(8,128)S(1)} %get-tuple-element.186), channel_id=1, source_target_pairs={{1,0},{2,1},{3,2},{4,3},{5,4},{6,5},{7,6},{8,7},{9,8},{10,9},{11,1... | collective-permute-start | bytes 589832 | tf_op jit(solution)/shard_map/ppermute | solution.py:18
  163.7 6.9 %collective-permute-start.6 = (f32[1,3,128,128]{3,2,0,1:T(8,128)S(1)}, f32[1,3,128,128]{3,2,0,1:T(8,128)S(1)}, u32[]{:S(2)}, u32[]{:S(2)}) collective-permute-start(f32[1,3,128,128]{3,2,0,1:T(8,128)S(1)} %get-tuple-element.181), channel_id=1, source_target_pairs={{0,1},{1,2},{2,3},{3,4},{4,5},{5,6},{6,7},{7,8},{8,9},{9,10},{10,1... | collective-permute-start | bytes 589832 | tf_op jit(solution)/shard_map/ppermute | solution.py:18
  167.5 9.4 %collective-permute-start.7 = (f32[1,3,128,128]{3,2,0,1:T(8,128)S(1)}, f32[1,3,128,128]{3,2,0,1:T(8,128)S(1)}, u32[]{:S(2)}, u32[]{:S(2)}) collective-permute-start(f32[1,3,128,128]{3,2,0,1:T(8,128)S(1)} %get-tuple-element.182), channel_id=1, source_target_pairs={{1,0},{2,1},{3,2},{4,3},{5,4},{6,5},{7,6},{8,7},{9,8},{10,9},{11,1... | collective-permute-start | bytes 589832 | tf_op jit(solution)/shard_map/ppermute | solution.py:18
  194.9 6.4 %collective-permute-start.8 = (f32[1,3,128,128]{3,2,0,1:T(8,128)S(1)}, f32[1,3,128,128]{3,2,0,1:T(8,128)S(1)}, u32[]{:S(2)}, u32[]{:S(2)}) collective-permute-start(f32[1,3,128,128]{3,2,0,1:T(8,128)S(1)} %get-tuple-element.177), channel_id=1, source_target_pairs={{0,1},{1,2},{2,3},{3,4},{4,5},{5,6},{6,7},{7,8},{8,9},{9,10},{10,1... | collective-permute-start | bytes 589832 | tf_op jit(solution)/shard_map/ppermute | solution.py:18
  197.9 10.9 %collective-permute-start.9 = (f32[1,3,128,128]{3,2,0,1:T(8,128)S(1)}, f32[1,3,128,128]{3,2,0,1:T(8,128)S(1)}, u32[]{:S(2)}, u32[]{:S(2)}) collective-permute-start(f32[1,3,128,128]{3,2,0,1:T(8,128)S(1)} %get-tuple-element.178), channel_id=1, source_target_pairs={{1,0},{2,1},{3,2},{4,3},{5,4},{6,5},{7,6},{8,7},{9,8},{10,9},{11,1... | collective-permute-start | bytes 589832 | tf_op jit(solution)/shard_map/ppermute | solution.py:18
  226.6 6.5 %collective-permute-start.10 = (f32[1,3,128,128]{3,2,0,1:T(8,128)S(1)}, f32[1,3,128,128]{3,2,0,1:T(8,128)S(1)}, u32[]{:S(2)}, u32[]{:S(2)}) collective-permute-start(f32[1,3,128,128]{3,2,0,1:T(8,128)S(1)} %get-tuple-element.173), channel_id=1, source_target_pairs={{0,1},{1,2},{2,3},{3,4},{4,5},{5,6},{6,7},{7,8},{8,9},{9,10},{10,1... | collective-permute-start | bytes 589832 | tf_op jit(solution)/shard_map/ppermute | solution.py:18
  229.5 11.2 %collective-permute-start.11 = (f32[1,3,128,128]{3,2,0,1:T(8,128)S(1)}, f32[1,3,128,128]{3,2,0,1:T(8,128)S(1)}, u32[]{:S(2)}, u32[]{:S(2)}) collective-permute-start(f32[1,3,128,128]{3,2,0,1:T(8,128)S(1)} %get-tuple-element.174), channel_id=1, source_target_pairs={{1,0},{2,1},{3,2},{4,3},{5,4},{6,5},{7,6},{8,7},{9,8},{10,9},{11,1... | collective-permute-start | bytes 589832 | tf_op jit(solution)/shard_map/ppermute | solution.py:18
  266.8 12.8 %all-to-all-start.1 = ((f32[3,32,128]{2,0,1:T(4,128)}), f32[3,32,128]{2,0,1:T(4,128)S(1)}, u32[]{:S(2)}, u32[]{:S(2)}) async-start(f32[3,32,128]{2,0,1:T(4,128)} %copy.56), calls=%async_computation.1 | async-start | bytes 131072 | tf_op jit(solution)/shard_map/all_to_all | solution.py:107
  (65 other events, 1355.3 us)
where the time goes:
time: 311 us; the launch traced here: 305 us
  matrix products  106 us (34%)
  other arithmetic  67.9 us (22%)
  starting transfers between devices  47.6 us (15%)
  waiting for transfers between devices  47.2 us (15%)
  local copies, waits for them, and re-layouts  33.9 us (11%)
    dot_general x84, matrix products, band_product(): jnp.einsum('rpk,rkq->rpq', left_band[:, window_row], extended[window_row:...  106 us
    ppermute x12, waiting for transfers between devices, passed_along(): return lax.ppermute(value, axis, pairs)  35.3 us
    ppermute x12, starting transfers between devices, passed_along(): return lax.ppermute(value, axis, pairs)  28.5 us
    reduce_sum x9, other arithmetic, pair_force(): jnp.sum(weight_pair * component, axis=-1)  26.9 us
    scatter-add x1, other arithmetic, per_device(): empty.at[:, atom_list.reshape(-1)].add(returned.reshape(3, -1))  22.5 us
    gather x2, local copies, waits for them, and re-layouts, per_device(): chosen = jnp.take(payload, atom_list, axis=1)  17.4 us
    ppermute x3, starting transfers between devices, padded(): lax.ppermute(head, axis, [((i + 1) % count, i) for i in range(count)])  8.48 us
    squeeze x2, local copies, waits for them, and re-layouts, per_device(): diag_mean = jnp.mean(jnp.diagonal(current[:, W], axis1=1, axis2=2), axis=1)  7.03 us
  transfers between devices with their start and end apart: 20, of which 15 were waited for; matrix products, arithmetic and copies ran while one was open for 21% of the time, Pallas kernels for 0%

commit v1 on v0

v1 whole, which is shorter than its diff:
```python
import functools
import math

import jax
import jax.numpy as jnp
from jax import lax
from jax.experimental import pallas as pl
from jax.experimental.pallas import tpu as pltpu
from jax.sharding import PartitionSpec as P

W = 1
ITERS = 6


SIGMA_SQ = 0.25
EMBED = 20.0
SOFTEN = 1.0
MESH = pl.DeviceIdType.MESH
SCALE = math.sqrt(1.0 / (SIGMA_SQ * math.log(2.0)))


def padded(cells, sides, width):
    for axis, dim in sides:
        count = lax.axis_size(axis)
        head = lax.slice_in_dim(cells, 0, width, axis=dim)
        tail = lax.slice_in_dim(cells, cells.shape[dim] - width, cells.shape[dim], axis=dim)
        cells = jnp.concatenate(
            [
                lax.ppermute(tail, axis, [(i, (i + 1) % count) for i in range(count)]),
                cells,
                lax.ppermute(head, axis, [((i + 1) % count, i) for i in range(count)]),
            ],
            axis=dim,
        )
    return cells


def keep_of(pattern, first_row, total_rows):
    row_ids = first_row + jnp.arange(pattern.shape[0], dtype=jnp.int32)[:, None]
    column_ids = row_ids + jnp.arange(pattern.shape[1], dtype=jnp.int32)[None, :] - W
    inside = (column_ids >= 0) & (column_ids < total_rows) & (pattern > 0)
    return jnp.where(inside, 1.0, 0.0).astype(jnp.float32)


def split(value):
    high = value.astype(jnp.bfloat16)
    return high, (value - high.astype(jnp.float32)).astype(jnp.bfloat16)


def purify_kernel(
    sizes, keep_ref, density_ref, out_ref, diag_ref, high, low, outbox, inbox, send_sem, recv_sem
):
    rows, bs = density_ref.shape[0], density_ref.shape[2]
    n_col, n_grp = sizes[1], sizes[2]
    total = sizes[0] * n_col * n_grp
    me = (lax.axis_index("qrow") * n_col + lax.axis_index("qcol")) * n_grp + lax.axis_index("grp")
    has_prev, has_next = me > 0, me < total - 1

    def place(index):
        return (index // (n_col * n_grp), (index // n_grp) % n_col, index % n_grp)

    to_prev, to_next = place(jnp.maximum(me - 1, 0)), place(jnp.minimum(me + 1, total - 1))

    def copy_prev(s):
        return pltpu.make_async_remote_copy(
            outbox.at[s, 0], inbox.at[s, 1], send_sem.at[s, 0], recv_sem.at[s, 1],
            device_id=to_prev, device_id_type=MESH)

    def copy_next(s):
        return pltpu.make_async_remote_copy(
            outbox.at[s, 1], inbox.at[s, 0], send_sem.at[s, 1], recv_sem.at[s, 0],
            device_id=to_next, device_id_type=MESH)

    barrier = pltpu.get_barrier_semaphore()

    @pl.when(has_prev)
    def _():
        pl.semaphore_signal(barrier, inc=1, device_id=to_prev, device_id_type=MESH)

    @pl.when(has_next)
    def _():
        pl.semaphore_signal(barrier, inc=1, device_id=to_next, device_id_type=MESH)

    def masked(i):
        return jnp.concatenate([density_ref[i, e] * keep_ref[i, e] for e in range(3)], axis=1)

    def put(slot, row, value):
        high[slot, row], low[slot, row] = split(value)

    first, last = masked(0), masked(rows - 1)
    outbox[0, 0] = first
    outbox[0, 1] = last
    put(0, 1, first)
    put(0, rows, last)

    pl.semaphore_wait(barrier, jnp.where(has_prev, 1, 0) + jnp.where(has_next, 1, 0))

    def send(s):
        @pl.when(has_prev)
        def _():
            copy_prev(s).start()

        @pl.when(has_next)
        def _():
            copy_next(s).start()

    send(0)
    edge = jnp.zeros((bs, 3 * bs), jnp.bfloat16)
    for slot in range(2):
        for row in (0, rows + 1):
            high[slot, row] = edge
            low[slot, row] = edge

    def fill(i, carry):
        put(0, i + 1, masked(i))
        return carry

    lax.fori_loop(1, rows - 1, fill, 0)

    def product(left, windows):
        left_high, left_low = left
        parts = []
        for tile in range(2):
            columns = slice(tile * bs, (tile + 2) * bs)
            wide_high, wide_low = windows[tile]
            both = jnp.concatenate([left_high[:, columns], left_low[:, columns]], axis=0)
            by_high = jnp.dot(both, wide_high, preferred_element_type=jnp.float32)
            by_low = jnp.dot(left_high[:, columns], wide_low, preferred_element_type=jnp.float32)
            parts.append(by_high[:bs] + (by_high[bs:] + by_low))
        return [parts[0][:, :bs], parts[0][:, bs:] + parts[1][:, :bs], parts[1][:, bs:]]

    def window(store, slot, i):
        before, here, after = store.at[slot, i], store.at[slot, i + 1], store.at[slot, i + 2]
        one = jnp.concatenate([before[:, bs:], here[:, : 2 * bs]], axis=0)
        none = jnp.zeros((bs, bs), jnp.bfloat16)
        top = jnp.concatenate([none, here[:, 2 * bs :]], axis=1)
        return one, jnp.concatenate([top, after[:, : 2 * bs]], axis=0)

    def one_row(slot, i):
        windows = list(zip(window(high, slot, i), window(low, slot, i)))
        keep = [keep_ref[i, e] for e in range(3)]
        square = [keep[e] * block for e, block in enumerate(product((high[slot, i + 1], low[slot, i + 1]), windows))]
        square = jnp.concatenate(square, axis=1)
        cube = product(split(square), windows)
        fresh = [3.0 * square[:, e * bs : (e + 1) * bs] - (2.0 * keep[e]) * cube[e] for e in range(3)]
        for e in range(3):
            out_ref[i, e] = fresh[e]
        fresh = jnp.concatenate(fresh, axis=1)
        put(1 - slot, i + 1, fresh)
        return fresh

    middle = rows // 2

    def sweep(s, carry):
        slot = lax.rem(s, 2)

        def inner(i, c):
            one_row(slot, i)
            return c

        lax.fori_loop(1, middle, inner, 0, unroll=UNROLL_A)

        @pl.when(has_prev)
        def _():
            copy_prev(s).wait_send()
            copy_next(s).wait_recv()
            put(slot, 0, inbox[s, 0])

        @pl.when(has_next)
        def _():
            copy_next(s).wait_send()
            copy_prev(s).wait_recv()
            put(slot, rows + 1, inbox[s, 1])

        top = one_row(slot, 0)
        bottom = one_row(slot, rows - 1)

        @pl.when(s < ITERS - 1)
        def _():
            outbox[s + 1, 0] = top
            outbox[s + 1, 1] = bottom
            send(s + 1)

        lax.fori_loop(middle, rows - 1, inner, 0, unroll=UNROLL_A)
        return carry

    lax.fori_loop(0, ITERS, sweep, 0)
    eye = lax.broadcasted_iota(jnp.int32, (bs, bs), 0) == lax.broadcasted_iota(jnp.int32, (bs, bs), 1)

    def diagonal(i, carry):
        diag_ref[i] = jnp.sum(jnp.where(eye, out_ref[i, W], 0.0), axis=0, keepdims=True)
        return carry

    lax.fori_loop(0, rows, diagonal, 0)


UNROLL_A = 1


def purify(density, keep_mask, sizes):
    rows, band, bs = density.shape[:3]
    vmem, smem = pl.BlockSpec(memory_space=pltpu.VMEM), pl.BlockSpec(memory_space=pltpu.SMEM)
    return pl.pallas_call(
        functools.partial(purify_kernel, sizes),
        out_shape=(
            jax.ShapeDtypeStruct(density.shape, jnp.float32),
            jax.ShapeDtypeStruct((rows, 1, bs), jnp.float32),
        ),
        in_specs=[smem, vmem],
        out_specs=(vmem, vmem),
        scratch_shapes=[
            pltpu.VMEM((2, rows + 2, bs, band * bs), jnp.bfloat16),
            pltpu.VMEM((2, rows + 2, bs, band * bs), jnp.bfloat16),
            pltpu.VMEM((ITERS, 2, bs, band * bs), jnp.float32),
            pltpu.VMEM((ITERS, 2, bs, band * bs), jnp.float32),
            pltpu.SemaphoreType.DMA((ITERS, 2)),
            pltpu.SemaphoreType.DMA((ITERS, 2)),
        ],
        compiler_params=pltpu.CompilerParams(
            collective_id=0, has_side_effects=True, vmem_limit_bytes=40 * 1024 * 1024
        ),
        cost_estimate=pl.CostEstimate(
            flops=2 * 3 * 8 * 2 * ITERS * rows * bs**3, bytes_accessed=8 * density.size, transcendentals=0
        ),
    )(keep_mask, density)


def pair_kernel(cells, around_ref, own_ref, strength_ref, out_ref, spread):
    cells_x, cells_y, cells_z = cells
    atoms = own_ref.shape[2]
    step_y = cells_z + 2
    step_x = step_y * (cells_y + 2)
    ones = jnp.ones((8, atoms), jnp.float32)
    group = 32

    def one_cell(cell, carry):
        cx, cy, cz = cell // (cells_y * cells_z), (cell // cells_z) % cells_y, cell % cells_z
        corner = cx * step_x + cy * step_y + cz
        for axis in range(3):
            row = own_ref[axis, pl.ds(cell, 1), :]
            spread[axis] = jnp.transpose(jnp.broadcast_to(row, (atoms, atoms)))

        def one_group(g, c):
            here = pl.ds(pl.multiple_of(g * group, group), group)
            mine = [spread[axis, here, :] for axis in range(3)]
            sums = [jnp.zeros((group, atoms), jnp.float32) for _ in range(3)]
            for dx in range(3):
                for dy in range(3):
                    for dz in range(3):
                        at = pl.ds(corner + dx * step_x + dy * step_y + dz, 1)
                        gap = [mine[axis] - around_ref[axis, at, :] for axis in range(3)]
                        power = around_ref[3, at, :] - (gap[0] * gap[0] + gap[1] * gap[1] + gap[2] * gap[2])
                        weight = jnp.exp2(power)
                        sums = [sums[axis] + weight * gap[axis] for axis in range(3)]
            for axis in range(3):
                spread[3 + axis, here, :] = sums[axis]
            return c

        lax.fori_loop(0, atoms // group, one_group, 0)
        strength = strength_ref[pl.ds(cell, 1), :] * (1.0 / SCALE)
        for axis in range(3):
            summed = lax.dot_general(
                ones, spread[3 + axis], (((1,), (1,)), ((), ())),
                precision=lax.Precision.HIGHEST, preferred_element_type=jnp.float32)
            out_ref[axis, pl.ds(cell, 1), :] = summed[:1] * strength
        return carry

    lax.fori_loop(0, cells_x * cells_y * cells_z, one_cell, 0)


def embed_kernel(per_owner, list_ref, table_ref, coords_ref, charge_ref, pair_ref, out_ref):
    cells, atoms = charge_ref.shape
    slots = list_ref.shape[1]
    cell_ids = lax.broadcasted_iota(jnp.int32, (16, slots), 0)
    atom_ids = lax.broadcasted_iota(jnp.int32, (atoms, slots), 0)

    def one_owner(owner, sums):
        row = list_ref[pl.ds(owner, 1), :]
        in_cell = jnp.where(cell_ids == (row >> int(math.log2(atoms))), 1.0, 0.0).astype(jnp.bfloat16)
        in_slot = jnp.where(atom_ids == (row & (atoms - 1)), 1.0, 0.0).astype(jnp.bfloat16)
        times = lax.dot_general(in_cell, in_slot, (((1,), (1,)), ((), ())), preferred_element_type=jnp.float32)
        sums = list(sums)
        for part in range(per_owner // 8):
            start = pl.ds(pl.multiple_of(owner * per_owner + part * 8, 8), 8)
            table = table_ref[start, :]
            site = [jnp.broadcast_to(table[:, k : k + 1], (8, atoms)) for k in range(4)]
            for cell in range(cells):
                gap = [coords_ref[axis, cell : cell + 1, :] - site[axis] for axis in range(3)]
                square = gap[0] * gap[0] + gap[1] * gap[1] + gap[2] * gap[2] + SOFTEN
                root = lax.rsqrt(square)
                factor = (site[3] * times[cell : cell + 1, :]) * (root * root * root)
                for axis in range(3):
                    sums[axis * cells + cell] = sums[axis * cells + cell] + factor * gap[axis]
        return tuple(sums)

    zero = jnp.zeros((8, atoms), jnp.float32)
    sums = lax.fori_loop(0, list_ref.shape[0], one_owner, (zero,) * (3 * cells))
    for axis in range(3):
        for cell in range(cells):
            force = jnp.sum(sums[axis * cells + cell], axis=0, keepdims=True)
            out_ref[axis, cell : cell + 1, :] = (
                pair_ref[axis, cell : cell + 1, :] + EMBED * charge_ref[cell : cell + 1, :] * force
            )


def per_device(
    density, pattern, qm_sites, positions, atom_types, charges, eps_table, embed_atoms, embed_counts
):
    row_count = density.shape[0]
    axes = ("qrow", "qcol", "grp")
    sizes = tuple(lax.axis_size(axis) for axis in axes)
    device_count = sizes[0] * sizes[1] * sizes[2]
    first_row = lax.axis_index(axes) * row_count
    keep_mask = keep_of(pattern, first_row, row_count * device_count)
    grid_shape = positions.shape[1:]
    cells, atoms = grid_shape[:3], grid_shape[3]
    cell_count = cells[0] * cells[1] * cells[2]
    flat = (cell_count, atoms)

    type_ids = jnp.arange(eps_table.shape[0], dtype=jnp.int32)[:, None, None, None, None]
    strength = jnp.sqrt(
        jnp.sum(
            jnp.where(atom_types[None] == type_ids, eps_table[:, None, None, None, None], 0.0),
            axis=0,
        )
    )
    stacked = jnp.concatenate([positions, jnp.log2(strength)[None]], axis=0)
    extended = padded(stacked, (("qrow", 1), ("qcol", 2), ("grp", 3)), 1)
    wide = extended.shape[1:]
    around = jnp.concatenate(
        [
            jnp.stack(
                [
                    (extended[axis] + (lax.broadcasted_iota(jnp.int32, wide, axis) - 1).astype(jnp.float32)) * SCALE
                    for axis in range(3)
                ]
            ),
            extended[3:],
        ],
        axis=0,
    ).reshape(4, -1, atoms)
    local = [lax.broadcasted_iota(jnp.int32, grid_shape, axis) for axis in range(3)]
    own = jnp.stack([(positions[axis] + local[axis].astype(jnp.float32)) * SCALE for axis in range(3)])
    coords = jnp.stack(
        [
            positions[axis] + (local[axis] + lax.axis_index(axes[axis]) * cells[axis]).astype(jnp.float32)
            for axis in range(3)
        ]
    ).reshape((3,) + flat)

    current, diagonal = purify(density, keep_mask, sizes)
    qm_charge = qm_sites[3] - jnp.mean(diagonal[:, 0], axis=1)
    table = jnp.concatenate([qm_sites[:3], qm_charge[None]], axis=0).T
    table = lax.all_gather(table, axes, axis=0, tiled=True)

    pair = pl.pallas_call(
        functools.partial(pair_kernel, cells),
        out_shape=jax.ShapeDtypeStruct((3,) + flat, jnp.float32),
        scratch_shapes=[pltpu.VMEM((6, atoms, atoms), jnp.float32)],
        compiler_params=pltpu.CompilerParams(vmem_limit_bytes=16 * 1024 * 1024),
        cost_estimate=pl.CostEstimate(
            flops=27 * 15 * cell_count * atoms * atoms, bytes_accessed=4 * around.size,
            transcendentals=27 * cell_count * atoms * atoms,
        ),
    )(around, own.reshape((3,) + flat), strength.reshape(flat))

    live = jnp.arange(embed_atoms.shape[2], dtype=jnp.int32)[None, :] < embed_counts[0][:, None]
    lists = jnp.where(live, embed_atoms[0], -1)
    force = pl.pallas_call(
        functools.partial(embed_kernel, row_count),
        out_shape=jax.ShapeDtypeStruct((3,) + flat, jnp.float32),
        compiler_params=pltpu.CompilerParams(vmem_limit_bytes=16 * 1024 * 1024),
    )(lists, table, coords, charges.reshape(flat), pair)
    return (current, force.reshape(positions.shape))


def solution(mesh):
    in_specs = (
        P(("qrow", "qcol", "grp"), None, None, None),
        P(("qrow", "qcol", "grp"), None),
        P(None, ("qrow", "qcol", "grp")),
        P(None, "qrow", "qcol", "grp", None),
        P("qrow", "qcol", "grp", None),
        P("qrow", "qcol", "grp", None),
        P(),
        P(("qrow", "qcol", "grp"), None, None),
        P(("qrow", "qcol", "grp"), None),
    )
    out_specs = (P(("qrow", "qcol", "grp"), None, None, None), P(None, "qrow", "qcol", "grp", None))
    return jax.shard_map(
        per_device, mesh=mesh, in_specs=in_specs, out_specs=out_specs, check_vma=False
    )
```

time: 311 us -> 176 us (0.57); the launches traced: 305 us -> 176 us
  matrix products: 106 us -> 0 us
  Pallas kernels: 0 us -> 84.3 us
  other arithmetic: 67.9 us -> 3.05 us
  blocking collectives: 0 us -> 63.7 us
  waiting for transfers between devices: 47.2 us -> 5.53 us
  starting transfers between devices: 47.6 us -> 13.4 us
  local copies, waits for them, and re-layouts: 33.9 us -> 5.3 us
    dot_general x84 -> x0, matrix products: 106 us -> none  [band_product(): jnp.einsum('rpk,rkq->rpq', left_band[:, window_row], extended[window_row:...]
    pallas_call x0 -> x3, Pallas kernels: none -> 84.3 us  [the longest x1 65 us: purify(): pl.pallas_call(functools.partial(purify_kernel, sizes), out_shape=(jax.Sh...]
    all_gather x0 -> x1, blocking collectives: none -> 63.7 us  [per_device(): table = lax.all_gather(table, axes, axis=0, tiled=True)]
    ppermute x12 -> x0, waiting for transfers between devices: 35.3 us -> none  [passed_along(): return lax.ppermute(value, axis, pairs)]
    ppermute x12 -> x0, starting transfers between devices: 28.5 us -> none  [passed_along(): return lax.ppermute(value, axis, pairs)]
    reduce_sum x11 -> x1, other arithmetic: 27.4 us -> 0.2 us  [per_device(): qm_charge = qm_sites[3] - jnp.mean(diagonal[:, 0], axis=1)]
    scatter-add x1 -> x0, other arithmetic: 22.5 us -> none  [per_device(): empty.at[:, atom_list.reshape(-1)].add(returned.reshape(3, -1))]
    gather x3 -> x0, local copies, waits for them, and re-layouts: 19.2 us -> none  [the longest x2 17.4 us: per_device(): chosen = jnp.take(payload, atom_list, axis=1)]
  transfers between devices with their start and end apart: 20 -> 6, of which waited for: 15 -> 2; matrix products, arithmetic and copies ran while one was open for 21% -> 1% of each run, Pallas kernels for 0% -> 37%
where the time goes in v1:
time: 176 us
  Pallas kernels  84.3 us (48%)
  blocking collectives  63.7 us (36%)
  starting transfers between devices  13.4 us (8%)
  waiting for transfers between devices  5.53 us (3%)
  local copies, waits for them, and re-layouts  5.3 us (3%)
  other arithmetic  3.05 us (2%)
    pallas_call x1, Pallas kernels, purify(): pl.pallas_call(functools.partial(purify_kernel, sizes), out_shape=(jax.Sh...  65 us
    all_gather x1, blocking collectives, per_device(): table = lax.all_gather(table, axes, axis=0, tiled=True)  63.7 us
    pallas_call x1, Pallas kernels, per_device(): pl.pallas_call(functools.partial(pair_kernel, cells), out_shape=jax.Shape...  13 us
    ppermute x3, starting transfers between devices, padded(): lax.ppermute(head, axis, [((i + 1) % count, i) for i in range(count)])  11.3 us
    pallas_call x1, Pallas kernels, per_device(): pl.pallas_call(functools.partial(embed_kernel, row_count), out_shape=jax....  6.34 us
    unnamed x18, local copies, waits for them, and re-layouts  4.34 us
    ppermute x3, waiting for transfers between devices, padded(): lax.ppermute(tail, axis, [(i, (i + 1) % count) for i in range(count)])  4.1 us
  transfers between devices with their start and end apart: 6, of which 2 were waited for; matrix products, arithmetic and copies ran while one was open for 1% of the time, Pallas kernels for 37%

profile of v1, /device:TPU:0, one launch (start us, length us, event | category | flops | bytes accessed | tf_op | source)
XLA Modules:
  0.0 176.0 jit_solution(13100068921252251916)
XLA Ops:
  0.6 0.8 select_reduce_fusion
  1.4 0.7 fusion.3
  2.2 2.4 %collective-permute-start.1 = (f32[4,1,2,2,128]{4,3,2,1,0:T(2,128)S(1)}, f32[4,1,2,2,128]{4,3,2,1,0:T(2,128)S(1)}, u32[]{:S(2)}, u32[]{:S(2)}) collective-permute-start(f32[4,1,2,2,128]{4,3,2,1,0:T(2,128)S(1)} %get-tuple-element.15), channel_id=1, source_target_pairs={{8,0},{16,8},{24,16},{0,24},{9,1},{17,9},{25,17},{1,25},{10,2},{18... | collective-permute-start | bytes 24584 | tf_op jit(solution)/shard_map/ppermute | solution.py:31
  4.6 0.0 collective-permute-start
  4.6 0.8 copy.15
  5.4 0.1 fusion.8.keep_ref
  5.4 1.9 %copy-done.1 = f32[16,3,128,128]{3,2,1,0:T(8,128)S(1)} copy-done((f32[16,3,128,128]{3,2,1,0:T(8,128)S(1)}, f32[16,3,128,128]{3,2,1,0:T(8,128)}, u32[]{:S(2)}) %copy-start.1) | copy-done | bytes 3145752
  7.3 65.0 %shard_map.104 = (f32[16,3,128,128]{3,2,1,0:T(8,128)S(1)}, f32[16,1,128]{2,1,0:T(1,128)S(1)}) custom-call(f32[16,3]{1,0:T(8,128)S(1)} %fusion.8.keep_ref, f32[16,3,128,128]{3,2,1,0:T(8,128)S(1)} %copy-done.1), custom_call_target="tpu_custom_call" | custom-call | flops 19327352832 | bytes 6291456 | tf_op jit(solution)/shard_map/pallas_call | solution.py:203
  72.3 0.1 bitcast_select_fusion.list_ref
  72.4 0.2 reduce_sum.18
  72.6 0.1 add_multiply_fusion.2
  72.8 8.9 %collective-permute-start.3 = (f32[4,4,1,2,128]{4,3,2,1,0:T(2,128)S(1)}, f32[4,4,1,2,128]{4,3,2,1,0:T(2,128)S(1)}, u32[]{:S(2)}, u32[]{:S(2)}) collective-permute-start(f32[4,4,1,2,128]{4,3,2,1,0:T(2,128)S(1)} %get-tuple-element.13), channel_id=1, source_target_pairs={{2,0},{4,2},{6,4},{0,6},{3,1},{5,3},{7,5},{1,7},{10,8},{12,10},{14... | collective-permute-start | bytes 49160 | tf_op jit(solution)/shard_map/ppermute | solution.py:31
  81.7 1.4 collective-permute-done.3
  83.2 4.1 %collective-permute-done.2 = f32[4,4,1,2,128]{4,3,2,1,0:T(2,128)S(1)} collective-permute-done((f32[4,4,1,2,128]{4,3,2,1,0:T(2,128)S(1)}, f32[4,4,1,2,128]{4,3,2,1,0:T(2,128)S(1)}, u32[]{:S(2)}, u32[]{:S(2)}) %collective-permute-start.2) | collective-permute-done | bytes 16416 | tf_op jit(solution)/shard_map/ppermute | solution.py:29
  87.3 0.7 fusion.9
  88.0 2.0 %collective-permute-start.4 = (f32[4,4,4,1,128]{4,3,2,1,0:T(1,128)}, f32[4,4,4,1,128]{4,3,2,1,0:T(1,128)}, u32[]{:S(2)}, u32[]{:S(2)}) collective-permute-start(f32[4,4,4,1,128]{4,3,2,1,0:T(1,128)} %get-tuple-element.10), channel_id=1, source_target_pairs={{0,1},{1,0},{2,3},{3,2},{4,5},{5,4},{6,7},{7,6},{8,9},{9,8},{10,11... | collective-permute-start | bytes 98312 | tf_op jit(solution)/shard_map/ppermute | solution.py:29
  90.0 63.7 %all-gather = f32[32,16,4]{1,2,0:T(4,128)S(1)} all-gather(f32[1,16,4]{1,2,0:T(4,128)S(1)} %maximum_bitcast_fusion), channel_id=1, replica_groups=mesh['qrow'=4,'qcol'=4,'grp'=2] {'qrow','qcol','grp'}, dimensions={0}, use_global_device_ids=true | all-gather | bytes 8448 | tf_op jit(solution)/shard_map/all_gather | solution.py:354
  153.7 0.3 copy.16
  154.0 0.9 pad_maximum_fusion
  154.9 0.1 fusion.2
  155.0 0.0 copy-start
  155.0 13.0 %shard_map.105.pair_ref = f32[3,8,128]{2,1,0:T(8,128)S(1)} custom-call(f32[4,64,128]{2,1,0:T(8,128)S(1)} %pad_maximum_fusion.1.around_ref, f32[3,8,128]{2,1,0:T(8,128)S(1)} %pad_maximum_fusion.5.own_ref, f32[8,128]{1,0:T(8,128)S(1)} %bitcast.28), custom_call_target="tpu_custom_call" | custom-call | flops 53084160 | bytes 131072 | tf_op jit(solution)/shard_map/pallas_call | solution.py:356
  168.0 6.3 %shard_map.106 = f32[3,8,128]{2,1,0:T(8,128)} custom-call(s32[32,128]{1,0:T(8,128)S(1)} %bitcast_select_fusion.list_ref, f32[512,4]{1,0:T(8,128)S(1)} %bitcast.26, f32[3,8,128]{2,1,0:T(8,128)S(1)} %pad_maximum_fusion.4.coords_ref, f32[8,128]{1,0:T(8,128)S(1)} %bitcast.27, f32[3,8,128]{2,1,0:T(8,128)S(1)} %shard_map.105.pair_ref), custom_call_target="tpu_custom_call" | custom-call | tf_op jit(solution)/shard_map/pallas_call | solution.py:369
  174.3 1.7 copy.18
  (33 shorter events, 0.2 us)
Async XLA Ops:
  2.2 70.6 %collective-permute-start.1 = (f32[4,1,2,2,128]{4,3,2,1,0:T(2,128)S(1)}, f32[4,1,2,2,128]{4,3,2,1,0:T(2,128)S(1)}, u32[]{:S(2)}, u32[]{:S(2)}) collective-permute-start(f32[4,1,2,2,128]{4,3,2,1,0:T(2,128)S(1)} %get-tuple-element.15), channel_id=1, source_target_pairs={{8,0},{16,8},{24,16},{0,24},{9,1},{17,9},{25,17},{1,25},{10,2},{18... | collective-permute-start | bytes 24584 | tf_op jit(solution)/shard_map/ppermute | solution.py:31
  4.6 68.2 %collective-permute-start = (f32[4,1,2,2,128]{4,3,2,1,0:T(2,128)S(1)}, f32[4,1,2,2,128]{4,3,2,1,0:T(2,128)S(1)}, u32[]{:S(2)}, u32[]{:S(2)}) collective-permute-start(f32[4,1,2,2,128]{4,3,2,1,0:T(2,128)S(1)} %get-tuple-element.14), channel_id=1, source_target_pairs={{0,8},{8,16},{16,24},{24,0},{1,9},{9,17},{17,25},{25,1},{2,10},{10... | collective-permute-start | bytes 24584 | tf_op jit(solution)/shard_map/ppermute | solution.py:29
  5.4 1.9 %copy-start.1 = (f32[16,3,128,128]{3,2,1,0:T(8,128)S(1)}, f32[16,3,128,128]{3,2,1,0:T(8,128)}, u32[]{:S(2)}) copy-start(f32[16,3,128,128]{3,2,1,0:T(8,128)} %density_ref.1) | copy-start | bytes 9437188
  7.3 65.0 %copy-start.5 = (s32[1,32,128]{2,1,0:T(8,128)S(1)}, s32[1,32,128]{2,1,0:T(8,128)}, u32[]{:S(2)}) copy-start(s32[1,32,128]{2,1,0:T(8,128)} %param.16) | copy-start | bytes 49156
  7.3 65.0 %copy-start.7 = (s32[1,32]{1,0:T(1,128)S(1)}, s32[1,32]{1,0:T(1,128)}, u32[]{:S(2)}) copy-start(s32[1,32]{1,0:T(1,128)} %param.17) | copy-start | bytes 388
  7.3 65.3 %copy-start.6 = (f32[4,16]{1,0:T(4,128)S(1)}, f32[4,16]{1,0:T(4,128)}, u32[]{:S(2)}) copy-start(f32[4,16]{1,0:T(4,128)} %param.11) | copy-start | bytes 772
  7.3 65.3 %copy-start.2 = (f32[3,2,2,2,128]{4,3,2,1,0:T(2,128)S(1)}, f32[3,2,2,2,128]{4,3,2,1,0:T(2,128)}, u32[]{:S(2)}) copy-start(f32[3,2,2,2,128]{4,3,2,1,0:T(2,128)} %param.12) | copy-start | bytes 36868
  72.8 10.4 %collective-permute-start.3 = (f32[4,4,1,2,128]{4,3,2,1,0:T(2,128)S(1)}, f32[4,4,1,2,128]{4,3,2,1,0:T(2,128)S(1)}, u32[]{:S(2)}, u32[]{:S(2)}) collective-permute-start(f32[4,4,1,2,128]{4,3,2,1,0:T(2,128)S(1)} %get-tuple-element.13), channel_id=1, source_target_pairs={{2,0},{4,2},{6,4},{0,6},{3,1},{5,3},{7,5},{1,7},{10,8},{12,10},{14... | collective-permute-start | bytes 49160 | tf_op jit(solution)/shard_map/ppermute | solution.py:31
  81.7 5.5 %collective-permute-start.2 = (f32[4,4,1,2,128]{4,3,2,1,0:T(2,128)S(1)}, f32[4,4,1,2,128]{4,3,2,1,0:T(2,128)S(1)}, u32[]{:S(2)}, u32[]{:S(2)}) collective-permute-start(f32[4,4,1,2,128]{4,3,2,1,0:T(2,128)S(1)} %get-tuple-element.12), channel_id=1, source_target_pairs={{0,2},{2,4},{4,6},{6,0},{1,3},{3,5},{5,7},{7,1},{8,10},{10,12},{12... | collective-permute-start | bytes 49160 | tf_op jit(solution)/shard_map/ppermute | solution.py:29
  83.2 6.9 %copy-start.3 = (f32[4,4,1,2,128]{4,3,2,1,0:T(2,128)}, f32[4,4,1,2,128]{4,3,2,1,0:T(2,128)S(1)}, u32[]{:S(2)}) copy-start(f32[4,4,1,2,128]{4,3,2,1,0:T(2,128)S(1)} %collective-permute-done.3) | copy-start | bytes 49156
  87.3 2.8 %copy-start.4 = (f32[4,4,1,2,128]{4,3,2,1,0:T(2,128)}, f32[4,4,1,2,128]{4,3,2,1,0:T(2,128)S(1)}, u32[]{:S(2)}) copy-start(f32[4,4,1,2,128]{4,3,2,1,0:T(2,128)S(1)} %collective-permute-done.2) | copy-start | bytes 49156
  88.0 66.0 %collective-permute-start.5 = (f32[4,4,4,1,128]{4,3,2,1,0:T(1,128)}, f32[4,4,4,1,128]{4,3,2,1,0:T(1,128)}, u32[]{:S(2)}, u32[]{:S(2)}) collective-permute-start(f32[4,4,4,1,128]{4,3,2,1,0:T(1,128)} %get-tuple-element.11), channel_id=1, source_target_pairs={{1,0},{0,1},{3,2},{2,3},{5,4},{4,5},{7,6},{6,7},{9,8},{8,9},{11,10... | collective-permute-start | bytes 98312 | tf_op jit(solution)/shard_map/ppermute | solution.py:31
  88.0 66.0 %collective-permute-start.4 = (f32[4,4,4,1,128]{4,3,2,1,0:T(1,128)}, f32[4,4,4,1,128]{4,3,2,1,0:T(1,128)}, u32[]{:S(2)}, u32[]{:S(2)}) collective-permute-start(f32[4,4,4,1,128]{4,3,2,1,0:T(1,128)} %get-tuple-element.10), channel_id=1, source_target_pairs={{0,1},{1,0},{2,3},{3,2},{4,5},{5,4},{6,7},{7,6},{8,9},{9,8},{10,11... | collective-permute-start | bytes 98312 | tf_op jit(solution)/shard_map/ppermute | solution.py:29
  155.0 13.0 %copy-start = (f32[2,2,2,128]{3,2,1,0:T(2,128)S(1)}, f32[2,2,2,128]{3,2,1,0:T(2,128)}, u32[]{:S(2)}) copy-start(f32[2,2,2,128]{3,2,1,0:T(2,128)} %param.14) | copy-start | bytes 12292

commit v2 on v1

--- a/solution.py
+++ b/solution.py
@@ -16,6 +16,8 @@
 EMBED = 20.0
 SOFTEN = 1.0
 MESH = pl.DeviceIdType.MESH
+K_STACK = True
+AT_ONCE = 2
 SCALE = math.sqrt(1.0 / (SIGMA_SQ * math.log(2.0)))
 
 
@@ -81,8 +83,15 @@
     def _():
         pl.semaphore_signal(barrier, inc=1, device_id=to_next, device_id_type=MESH)
 
+    eye = lax.broadcasted_iota(jnp.int32, (bs, bs), 0) == lax.broadcasted_iota(jnp.int32, (bs, bs), 1)
+    half = jnp.where(eye, 0.5, 0.0)
+
     def masked(i):
-        return jnp.concatenate([density_ref[i, e] * keep_ref[i, e] for e in range(3)], axis=1)
+        blocks = [density_ref[i, e] * keep_ref[i, e] for e in range(3)]
+        blocks[W] = blocks[W] - half
+        for e in range(3):
+            out_ref[i, e] = blocks[e]
+        return jnp.concatenate(blocks, axis=1)
 
     def put(slot, row, value):
         high[slot, row], low[slot, row] = split(value)
@@ -123,10 +132,15 @@
         for tile in range(2):
             columns = slice(tile * bs, (tile + 2) * bs)
             wide_high, wide_low = windows[tile]
-            both = jnp.concatenate([left_high[:, columns], left_low[:, columns]], axis=0)
-            by_high = jnp.dot(both, wide_high, preferred_element_type=jnp.float32)
-            by_low = jnp.dot(left_high[:, columns], wide_low, preferred_element_type=jnp.float32)
-            parts.append(by_high[:bs] + (by_high[bs:] + by_low))
+            if K_STACK:
+                deep = jnp.concatenate([left_high[:, columns], left_low[:, columns], left_high[:, columns]], axis=1)
+                wide = jnp.concatenate([wide_high, wide_high, wide_low], axis=0)
+                parts.append(jnp.dot(deep, wide, preferred_element_type=jnp.float32))
+            else:
+                both = jnp.concatenate([left_high[:, columns], left_low[:, columns]], axis=0)
+                by_high = jnp.dot(both, wide_high, preferred_element_type=jnp.float32)
+                by_low = jnp.dot(left_high[:, columns], wide_low, preferred_element_type=jnp.float32)
+                parts.append(by_high[:bs] + (by_high[bs:] + by_low))
         return [parts[0][:, :bs], parts[0][:, bs:] + parts[1][:, :bs], parts[1][:, bs:]]
 
     def window(store, slot, i):
@@ -136,29 +150,35 @@
         top = jnp.concatenate([none, here[:, 2 * bs :]], axis=1)
         return one, jnp.concatenate([top, after[:, : 2 * bs]], axis=0)
 
-    def one_row(slot, i):
-        windows = list(zip(window(high, slot, i), window(low, slot, i)))
-        keep = [keep_ref[i, e] for e in range(3)]
-        square = [keep[e] * block for e, block in enumerate(product((high[slot, i + 1], low[slot, i + 1]), windows))]
-        square = jnp.concatenate(square, axis=1)
-        cube = product(split(square), windows)
-        fresh = [3.0 * square[:, e * bs : (e + 1) * bs] - (2.0 * keep[e]) * cube[e] for e in range(3)]
-        for e in range(3):
-            out_ref[i, e] = fresh[e]
-        fresh = jnp.concatenate(fresh, axis=1)
-        put(1 - slot, i + 1, fresh)
-        return fresh
-
-    middle = rows // 2
+    def some_rows(slot, picked):
+        windows = [list(zip(window(high, slot, i), window(low, slot, i))) for i in picked]
+        keeps = [[keep_ref[i, e] for e in range(3)] for i in picked]
+        squares = []
+        for i, pieces, keep in zip(picked, windows, keeps):
+            blocks = product((high[slot, i + 1], low[slot, i + 1]), pieces)
+            squares.append(split(jnp.concatenate([keep[e] * blocks[e] for e in range(3)], axis=1)))
+        cubes = [product(square, pieces) for square, pieces in zip(squares, windows)]
+        results = []
+        for i, cube, keep in zip(picked, cubes, keeps):
+            fresh = [1.5 * out_ref[i, e] - (2.0 * keep[e]) * cube[e] for e in range(3)]
+            results.append((fresh, split(jnp.concatenate(fresh, axis=1))))
+        for i, (fresh, (fresh_high, fresh_low)) in zip(picked, results):
+            for e in range(3):
+                out_ref[i, e] = fresh[e]
+            high[1 - slot, i + 1] = fresh_high
+            low[1 - slot, i + 1] = fresh_low
+        return [jnp.concatenate(fresh, axis=1) for fresh, _ in results]
+
+    steps = (rows - 2) // AT_ONCE
 
     def sweep(s, carry):
         slot = lax.rem(s, 2)
 
         def inner(i, c):
-            one_row(slot, i)
+            some_rows(slot, [1 + AT_ONCE * i + k for k in range(AT_ONCE)])
             return c
 
-        lax.fori_loop(1, middle, inner, 0, unroll=UNROLL_A)
+        lax.fori_loop(0, steps // 2, inner, 0)
 
         @pl.when(has_prev)
         def _():
@@ -172,8 +192,7 @@
             copy_prev(s).wait_recv()
             put(slot, rows + 1, inbox[s, 1])
 
-        top = one_row(slot, 0)
-        bottom = one_row(slot, rows - 1)
+        top, bottom = some_rows(slot, [0, rows - 1])
 
         @pl.when(s < ITERS - 1)
         def _():
@@ -181,20 +200,18 @@
             outbox[s + 1, 1] = bottom
             send(s + 1)
 
-        lax.fori_loop(middle, rows - 1, inner, 0, unroll=UNROLL_A)
+        lax.fori_loop(steps // 2, steps, inner, 0)
         return carry
 
     lax.fori_loop(0, ITERS, sweep, 0)
-    eye = lax.broadcasted_iota(jnp.int32, (bs, bs), 0) == lax.broadcasted_iota(jnp.int32, (bs, bs), 1)
 
     def diagonal(i, carry):
-        diag_ref[i] = jnp.sum(jnp.where(eye, out_ref[i, W], 0.0), axis=0, keepdims=True)
+        block = out_ref[i, W] + half
+        out_ref[i, W] = block
+        diag_ref[i] = jnp.sum(jnp.where(eye, block, 0.0), axis=0, keepdims=True)
         return carry
 
     lax.fori_loop(0, rows, diagonal, 0)
-
-
-UNROLL_A = 1
 
 
 def purify(density, keep_mask, sizes):
@@ -351,7 +368,9 @@
     current, diagonal = purify(density, keep_mask, sizes)
     qm_charge = qm_sites[3] - jnp.mean(diagonal[:, 0], axis=1)
     table = jnp.concatenate([qm_sites[:3], qm_charge[None]], axis=0).T
-    table = lax.all_gather(table, axes, axis=0, tiled=True)
+    table = lax.all_to_all(
+        jnp.broadcast_to(table.reshape(1, -1), (device_count, table.size)), axes, 0, 0, tiled=True
+    ).reshape(-1, 4)
 
     pair = pl.pallas_call(
         functools.partial(pair_kernel, cells),

time: 176 us -> 121 us (0.69)
  blocking collectives: 63.7 us -> 0 us
  waiting for transfers between devices: 5.53 us -> 10.7 us
  starting transfers between devices: 13.4 us -> 16.1 us
    all_gather x1 -> x0, blocking collectives: 63.7 us -> none  [per_device(): table = lax.all_gather(table, axes, axis=0, tiled=True)]
    all_to_all x0 -> x1, starting transfers between devices: none -> 9.15 us  [per_device(): lax.all_to_all(jnp.broadcast_to(table.reshape(1, -1), (device_count, tabl...]
    ppermute x3, starting transfers between devices: 11.3 us -> 6.44 us  [padded(): lax.ppermute(head, axis, [((i + 1) % count, i) for i in range(count)])]
    ppermute x3, waiting for transfers between devices: 4.1 us -> 7.31 us  [padded(): lax.ppermute(tail, axis, [(i, (i + 1) % count) for i in range(count)])]
    ppermute x3, waiting for transfers between devices: 1.44 us -> 3.43 us  [padded(): lax.ppermute(head, axis, [((i + 1) % count, i) for i in range(count)])]
  transfers between devices with their start and end apart: 6 -> 7, of which waited for: 2 -> 6; matrix products, arithmetic and copies ran while one was open for 1% -> 2% of each run, Pallas kernels for 37% -> 0%
where the time goes in v2:
time: 121 us; the launch traced here: 120 us
  Pallas kernels  83.9 us (69%)
  starting transfers between devices  16.1 us (13%)
  waiting for transfers between devices  10.7 us (9%)
  local copies, waits for them, and re-layouts  6.49 us (5%)
  other arithmetic  2.28 us (2%)
    pallas_call x1, Pallas kernels, purify(): pl.pallas_call(functools.partial(purify_kernel, sizes), out_shape=(jax.Sh...  64.6 us
    pallas_call x1, Pallas kernels, per_device(): pl.pallas_call(functools.partial(pair_kernel, cells), out_shape=jax.Shape...  13 us
    all_to_all x1, starting transfers between devices, per_device(): lax.all_to_all(jnp.broadcast_to(table.reshape(1, -1), (device_count, tabl...  9.15 us
    ppermute x3, waiting for transfers between devices, padded(): lax.ppermute(tail, axis, [(i, (i + 1) % count) for i in range(count)])  7.31 us
    ppermute x3, starting transfers between devices, padded(): lax.ppermute(head, axis, [((i + 1) % count, i) for i in range(count)])  6.44 us
    pallas_call x1, Pallas kernels, per_device(): pl.pallas_call(functools.partial(embed_kernel, row_count), out_shape=jax....  6.34 us
    unnamed x18, local copies, waits for them, and re-layouts  4.35 us
    ppermute x3, waiting for transfers between devices, padded(): lax.ppermute(head, axis, [((i + 1) % count, i) for i in range(count)])  3.43 us
  transfers between devices with their start and end apart: 7, of which 6 were waited for; matrix products, arithmetic and copies ran while one was open for 2% of the time, Pallas kernels for 0%

profile of v2, /device:TPU:0, one launch (start us, length us, event | category | flops | bytes accessed | tf_op | source)
XLA Modules:
  0.0 120.4 jit_solution(6470726350190726301)
XLA Ops:
  0.6 0.8 copy.17
  1.5 1.9 %copy-done.1 = f32[16,3,128,128]{3,2,1,0:T(8,128)S(1)} copy-done((f32[16,3,128,128]{3,2,1,0:T(8,128)S(1)}, f32[16,3,128,128]{3,2,1,0:T(8,128)}, u32[]{:S(2)}) %copy-start.1) | copy-done | bytes 3145752
  3.4 64.6 %shard_map.104 = (f32[16,3,128,128]{3,2,1,0:T(8,128)S(1)}, f32[16,1,128]{2,1,0:T(1,128)S(1)}) custom-call(f32[16,3]{1,0:T(8,128)S(1)} %fusion.8.keep_ref, f32[16,3,128,128]{3,2,1,0:T(8,128)S(1)} %copy-done.1), custom_call_target="tpu_custom_call" | custom-call | flops 19327352832 | bytes 6291456 | tf_op jit(solution)/shard_map/pallas_call | solution.py:220
  68.0 0.2 reduce_sum.18
  68.4 0.6 broadcast_in_dim.43
  69.0 9.1 %all-to-all-start = ((f32[32,1,64]{2,1,0:T(1,128)}), f32[32,1,64]{2,1,0:T(1,128)S(1)}, u32[]{:S(2)}, u32[]{:S(2)}) async-start(f32[32,1,64]{2,1,0:T(1,128)} %broadcast_in_dim.43), calls=%async_computation | async-start | bytes 32768 | tf_op jit(solution)/shard_map/all_to_all | solution.py:371
  78.3 1.6 %collective-permute-start.1 = (f32[4,1,2,2,128]{4,3,2,1,0:T(2,128)S(1)}, f32[4,1,2,2,128]{4,3,2,1,0:T(2,128)S(1)}, u32[]{:S(2)}, u32[]{:S(2)}) collective-permute-start(f32[4,1,2,2,128]{4,3,2,1,0:T(2,128)S(1)} %get-tuple-element.15), channel_id=1, source_target_pairs={{8,0},{16,8},{24,16},{0,24},{9,1},{17,9},{25,17},{1,25},{10,2},{18... | collective-permute-start | bytes 24584 | tf_op jit(solution)/shard_map/ppermute | solution.py:33
  80.1 1.2 collective-permute-done.1
  81.3 1.7 %collective-permute-done = f32[4,1,2,2,128]{4,3,2,1,0:T(2,128)S(1)} collective-permute-done((f32[4,1,2,2,128]{4,3,2,1,0:T(2,128)S(1)}, f32[4,1,2,2,128]{4,3,2,1,0:T(2,128)S(1)}, u32[]{:S(2)}, u32[]{:S(2)}) %collective-permute-start) | collective-permute-done | bytes 8224 | tf_op jit(solution)/shard_map/ppermute | solution.py:31
  83.0 3.4 %collective-permute-start.3 = (f32[4,4,1,2,128]{4,3,2,1,0:T(2,128)S(1)}, f32[4,4,1,2,128]{4,3,2,1,0:T(2,128)S(1)}, u32[]{:S(2)}, u32[]{:S(2)}) collective-permute-start(f32[4,4,1,2,128]{4,3,2,1,0:T(2,128)S(1)} %get-tuple-element.13), channel_id=1, source_target_pairs={{2,0},{4,2},{6,4},{0,6},{3,1},{5,3},{7,5},{1,7},{10,8},{12,10},{14... | collective-permute-start | bytes 49160 | tf_op jit(solution)/shard_map/ppermute | solution.py:33
  86.4 1.4 %collective-permute-done.3 = f32[4,4,1,2,128]{4,3,2,1,0:T(2,128)S(1)} collective-permute-done((f32[4,4,1,2,128]{4,3,2,1,0:T(2,128)S(1)}, f32[4,4,1,2,128]{4,3,2,1,0:T(2,128)S(1)}, u32[]{:S(2)}, u32[]{:S(2)}) %collective-permute-start.3) | collective-permute-done | bytes 16416 | tf_op jit(solution)/shard_map/ppermute | solution.py:33
  87.9 4.1 %collective-permute-done.2 = f32[4,4,1,2,128]{4,3,2,1,0:T(2,128)S(1)} collective-permute-done((f32[4,4,1,2,128]{4,3,2,1,0:T(2,128)S(1)}, f32[4,4,1,2,128]{4,3,2,1,0:T(2,128)S(1)}, u32[]{:S(2)}, u32[]{:S(2)}) %collective-permute-start.2) | collective-permute-done | bytes 16416 | tf_op jit(solution)/shard_map/ppermute | solution.py:31
  92.0 0.7 fusion.9
  92.7 1.5 %collective-permute-start.5 = (f32[4,4,4,1,128]{4,3,2,1,0:T(1,128)}, f32[4,4,4,1,128]{4,3,2,1,0:T(1,128)}, u32[]{:S(2)}, u32[]{:S(2)}) collective-permute-start(f32[4,4,4,1,128]{4,3,2,1,0:T(1,128)} %get-tuple-element.11), channel_id=1, source_target_pairs={{1,0},{0,1},{3,2},{2,3},{5,4},{4,5},{7,6},{6,7},{9,8},{8,9},{11,10... | collective-permute-start | bytes 98312 | tf_op jit(solution)/shard_map/ppermute | solution.py:33
  94.2 0.5 collective-permute-start.4
  94.7 0.5 broadcast.110
  95.2 0.7 reduce.4
  95.9 0.2 reshape.69.table_ref
  96.1 0.8 collective-permute-done.5
  96.9 1.5 %collective-permute-done.4 = f32[4,4,4,1,128]{4,3,2,1,0:T(1,128)} collective-permute-done((f32[4,4,4,1,128]{4,3,2,1,0:T(1,128)}, f32[4,4,4,1,128]{4,3,2,1,0:T(1,128)}, u32[]{:S(2)}, u32[]{:S(2)}) %collective-permute-start.4) | collective-permute-done | bytes 32800 | tf_op jit(solution)/shard_map/ppermute | solution.py:31
  98.4 0.9 pad_maximum_fusion
  99.4 13.0 %shard_map.105.pair_ref = f32[3,8,128]{2,1,0:T(8,128)S(1)} custom-call(f32[4,64,128]{2,1,0:T(8,128)S(1)} %pad_maximum_fusion.1.around_ref, f32[3,8,128]{2,1,0:T(8,128)S(1)} %pad_maximum_fusion.5.own_ref, f32[8,128]{1,0:T(8,128)S(1)} %bitcast.24), custom_call_target="tpu_custom_call" | custom-call | flops 53084160 | bytes 131072 | tf_op jit(solution)/shard_map/pallas_call | solution.py:375
  112.4 6.3 %shard_map.106 = f32[3,8,128]{2,1,0:T(8,128)} custom-call(s32[32,128]{1,0:T(8,128)S(1)} %bitcast_select_fusion.list_ref, f32[512,4]{1,0:T(8,128)S(1)} %reshape.69.table_ref, f32[3,8,128]{2,1,0:T(8,128)S(1)} %pad_maximum_fusion.4.coords_ref, f32[8,128]{1,0:T(8,128)S(1)} %bitcast.23, f32[3,8,128]{2,1,0:T(8,128)S(1)} %shard_map.105.pair_ref), custom_call_target="tpu_custom_call" | custom-call | tf_op jit(solution)/shard_map/pallas_call | solution.py:388
  118.7 1.7 %copy.20 = f32[16,3,128,128]{3,2,1,0:T(8,128)} copy(f32[16,3,128,128]{3,2,1,0:T(8,128)S(1)} %get-tuple-element.30) | data formatting | bytes 6291456
  (39 shorter events, 0.8 us)
Async XLA Ops:
  1.5 1.9 %copy-start.1 = (f32[16,3,128,128]{3,2,1,0:T(8,128)S(1)}, f32[16,3,128,128]{3,2,1,0:T(8,128)}, u32[]{:S(2)}) copy-start(f32[16,3,128,128]{3,2,1,0:T(8,128)} %density_ref.1) | copy-start | bytes 9437188
  3.4 64.8 %copy-start.5 = (f32[4,16]{1,0:T(4,128)S(1)}, f32[4,16]{1,0:T(4,128)}, u32[]{:S(2)}) copy-start(f32[4,16]{1,0:T(4,128)} %param.11) | copy-start | bytes 772
  3.4 74.8 %copy-start.4 = (s32[2,2,2,128]{3,2,1,0:T(2,128)S(1)}, s32[2,2,2,128]{3,2,1,0:T(2,128)}, u32[]{:S(2)}) copy-start(s32[2,2,2,128]{3,2,1,0:T(2,128)} %param.13) | copy-start | bytes 12292
  3.4 74.8 %copy-start.7 = (f32[8]{0:T(128)S(1)}, f32[8]{0:T(128)}, u32[]{:S(2)}) copy-start(f32[8]{0:T(128)} %param.15) | copy-start | bytes 100
  3.4 74.9 %copy-start.2 = (f32[3,2,2,2,128]{4,3,2,1,0:T(2,128)S(1)}, f32[3,2,2,2,128]{4,3,2,1,0:T(2,128)}, u32[]{:S(2)}) copy-start(f32[3,2,2,2,128]{4,3,2,1,0:T(2,128)} %param.12) | copy-start | bytes 36868
  3.4 76.5 %copy-start.3 = (s32[1,32,128]{2,1,0:T(8,128)S(1)}, s32[1,32,128]{2,1,0:T(8,128)}, u32[]{:S(2)}) copy-start(s32[1,32,128]{2,1,0:T(8,128)} %param.16) | copy-start | bytes 49156
  3.4 76.5 %copy-start.6 = (s32[1,32]{1,0:T(1,128)S(1)}, s32[1,32]{1,0:T(1,128)}, u32[]{:S(2)}) copy-start(s32[1,32]{1,0:T(1,128)} %param.17) | copy-start | bytes 388
  69.0 25.7 %all-to-all-start = ((f32[32,1,64]{2,1,0:T(1,128)}), f32[32,1,64]{2,1,0:T(1,128)S(1)}, u32[]{:S(2)}, u32[]{:S(2)}) async-start(f32[32,1,64]{2,1,0:T(1,128)} %broadcast_in_dim.43), calls=%async_computation | async-start | bytes 32768 | tf_op jit(solution)/shard_map/all_to_all | solution.py:371
  78.3 2.9 %collective-permute-start.1 = (f32[4,1,2,2,128]{4,3,2,1,0:T(2,128)S(1)}, f32[4,1,2,2,128]{4,3,2,1,0:T(2,128)S(1)}, u32[]{:S(2)}, u32[]{:S(2)}) collective-permute-start(f32[4,1,2,2,128]{4,3,2,1,0:T(2,128)S(1)} %get-tuple-element.15), channel_id=1, source_target_pairs={{8,0},{16,8},{24,16},{0,24},{9,1},{17,9},{25,17},{1,25},{10,2},{18... | collective-permute-start | bytes 24584 | tf_op jit(solution)/shard_map/ppermute | solution.py:33
  79.9 3.1 %collective-permute-start = (f32[4,1,2,2,128]{4,3,2,1,0:T(2,128)S(1)}, f32[4,1,2,2,128]{4,3,2,1,0:T(2,128)S(1)}, u32[]{:S(2)}, u32[]{:S(2)}) collective-permute-start(f32[4,1,2,2,128]{4,3,2,1,0:T(2,128)S(1)} %get-tuple-element.14), channel_id=1, source_target_pairs={{0,8},{8,16},{16,24},{24,0},{1,9},{9,17},{17,25},{25,1},{2,10},{10... | collective-permute-start | bytes 24584 | tf_op jit(solution)/shard_map/ppermute | solution.py:31
  83.0 4.8 %collective-permute-start.3 = (f32[4,4,1,2,128]{4,3,2,1,0:T(2,128)S(1)}, f32[4,4,1,2,128]{4,3,2,1,0:T(2,128)S(1)}, u32[]{:S(2)}, u32[]{:S(2)}) collective-permute-start(f32[4,4,1,2,128]{4,3,2,1,0:T(2,128)S(1)} %get-tuple-element.13), channel_id=1, source_target_pairs={{2,0},{4,2},{6,4},{0,6},{3,1},{5,3},{7,5},{1,7},{10,8},{12,10},{14... | collective-permute-start | bytes 49160 | tf_op jit(solution)/shard_map/ppermute | solution.py:33
  86.4 5.5 %collective-permute-start.2 = (f32[4,4,1,2,128]{4,3,2,1,0:T(2,128)S(1)}, f32[4,4,1,2,128]{4,3,2,1,0:T(2,128)S(1)}, u32[]{:S(2)}, u32[]{:S(2)}) collective-permute-start(f32[4,4,1,2,128]{4,3,2,1,0:T(2,128)S(1)} %get-tuple-element.12), channel_id=1, source_target_pairs={{0,2},{2,4},{4,6},{6,0},{1,3},{3,5},{5,7},{7,1},{8,10},{10,12},{12... | collective-permute-start | bytes 49160 | tf_op jit(solution)/shard_map/ppermute | solution.py:31
  92.7 4.2 %collective-permute-start.5 = (f32[4,4,4,1,128]{4,3,2,1,0:T(1,128)}, f32[4,4,4,1,128]{4,3,2,1,0:T(1,128)}, u32[]{:S(2)}, u32[]{:S(2)}) collective-permute-start(f32[4,4,4,1,128]{4,3,2,1,0:T(1,128)} %get-tuple-element.11), channel_id=1, source_target_pairs={{1,0},{0,1},{3,2},{2,3},{5,4},{4,5},{7,6},{6,7},{9,8},{8,9},{11,10... | collective-permute-start | bytes 98312 | tf_op jit(solution)/shard_map/ppermute | solution.py:33
  94.2 4.2 %collective-permute-start.4 = (f32[4,4,4,1,128]{4,3,2,1,0:T(1,128)}, f32[4,4,4,1,128]{4,3,2,1,0:T(1,128)}, u32[]{:S(2)}, u32[]{:S(2)}) collective-permute-start(f32[4,4,4,1,128]{4,3,2,1,0:T(1,128)} %get-tuple-element.10), channel_id=1, source_target_pairs={{0,1},{1,0},{2,3},{3,2},{4,5},{5,4},{6,7},{7,6},{8,9},{9,8},{10,11... | collective-permute-start | bytes 98312 | tf_op jit(solution)/shard_map/ppermute | solution.py:31
  99.4 13.0 %copy-start = (f32[2,2,2,128]{3,2,1,0:T(2,128)S(1)}, f32[2,2,2,128]{3,2,1,0:T(2,128)}, u32[]{:S(2)}) copy-start(f32[2,2,2,128]{3,2,1,0:T(2,128)} %param.14) | copy-start | bytes 12292

commit v3 on v2

--- a/solution.py
+++ b/solution.py
@@ -97,8 +97,8 @@
         high[slot, row], low[slot, row] = split(value)
 
     first, last = masked(0), masked(rows - 1)
-    outbox[0, 0] = first
-    outbox[0, 1] = last
+    outbox[0, 0] = first[:, : 2 * bs]
+    outbox[0, 1] = last[:, bs:]
     put(0, 1, first)
     put(0, rows, last)
 
@@ -184,20 +184,20 @@
         def _():
             copy_prev(s).wait_send()
             copy_next(s).wait_recv()
-            put(slot, 0, inbox[s, 0])
+            high[slot, 0, :, bs:], low[slot, 0, :, bs:] = split(inbox[s, 0])
 
         @pl.when(has_next)
         def _():
             copy_next(s).wait_send()
             copy_prev(s).wait_recv()
-            put(slot, rows + 1, inbox[s, 1])
+            high[slot, rows + 1, :, : 2 * bs], low[slot, rows + 1, :, : 2 * bs] = split(inbox[s, 1])
 
         top, bottom = some_rows(slot, [0, rows - 1])
 
         @pl.when(s < ITERS - 1)
         def _():
-            outbox[s + 1, 0] = top
-            outbox[s + 1, 1] = bottom
+            outbox[s + 1, 0] = top[:, : 2 * bs]
+            outbox[s + 1, 1] = bottom[:, bs:]
             send(s + 1)
 
         lax.fori_loop(steps // 2, steps, inner, 0)
@@ -228,8 +228,8 @@
         scratch_shapes=[
             pltpu.VMEM((2, rows + 2, bs, band * bs), jnp.bfloat16),
             pltpu.VMEM((2, rows + 2, bs, band * bs), jnp.bfloat16),
-            pltpu.VMEM((ITERS, 2, bs, band * bs), jnp.float32),
-            pltpu.VMEM((ITERS, 2, bs, band * bs), jnp.float32),
+            pltpu.VMEM((ITERS, 2, bs, (band - 1) * bs), jnp.float32),
+            pltpu.VMEM((ITERS, 2, bs, (band - 1) * bs), jnp.float32),
             pltpu.SemaphoreType.DMA((ITERS, 2)),
             pltpu.SemaphoreType.DMA((ITERS, 2)),
         ],

time: 121 us -> 106 us (0.88)
  Pallas kernels: 83.9 us -> 68.9 us
    pallas_call x1, Pallas kernels: 64.6 us -> 49.5 us  [purify(): pl.pallas_call(functools.partial(purify_kernel, sizes), out_shape=(jax.Sh...]
where the time goes in v3:
time: 106 us; the launch traced here: 105 us
  Pallas kernels  68.9 us (65%)
  starting transfers between devices  16.1 us (15%)
  waiting for transfers between devices  10.7 us (10%)
  local copies, waits for them, and re-layouts  6.49 us (6%)
  other arithmetic  2.28 us (2%)
    pallas_call x1, Pallas kernels, purify(): pl.pallas_call(functools.partial(purify_kernel, sizes), out_shape=(jax.Sh...  49.5 us
    pallas_call x1, Pallas kernels, per_device(): pl.pallas_call(functools.partial(pair_kernel, cells), out_shape=jax.Shape...  13 us
    all_to_all x1, starting transfers between devices, per_device(): lax.all_to_all(jnp.broadcast_to(table.reshape(1, -1), (device_count, tabl...  9.14 us
    ppermute x3, waiting for transfers between devices, padded(): lax.ppermute(tail, axis, [(i, (i + 1) % count) for i in range(count)])  7.31 us
    ppermute x3, starting transfers between devices, padded(): lax.ppermute(head, axis, [((i + 1) % count, i) for i in range(count)])  6.44 us
    pallas_call x1, Pallas kernels, per_device(): pl.pallas_call(functools.partial(embed_kernel, row_count), out_shape=jax....  6.34 us
    unnamed x18, local copies, waits for them, and re-layouts  4.35 us
    ppermute x3, waiting for transfers between devices, padded(): lax.ppermute(head, axis, [((i + 1) % count, i) for i in range(count)])  3.43 us
  transfers between devices with their start and end apart: 7, of which 6 were waited for; matrix products, arithmetic and copies ran while one was open for 2% of the time, Pallas kernels for 0%

profile of v3, /device:TPU:0, one launch (start us, length us, event | category | flops | bytes accessed | tf_op | source)
XLA Modules:
  0.0 105.3 jit_solution(12214918772891226335)
XLA Ops:
  0.6 0.8 copy.17
  1.5 1.9 %copy-done.1 = f32[16,3,128,128]{3,2,1,0:T(8,128)S(1)} copy-done((f32[16,3,128,128]{3,2,1,0:T(8,128)S(1)}, f32[16,3,128,128]{3,2,1,0:T(8,128)}, u32[]{:S(2)}) %copy-start.1) | copy-done | bytes 3145752
  3.4 49.5 %shard_map.104 = (f32[16,3,128,128]{3,2,1,0:T(8,128)S(1)}, f32[16,1,128]{2,1,0:T(1,128)S(1)}) custom-call(f32[16,3]{1,0:T(8,128)S(1)} %fusion.8.keep_ref, f32[16,3,128,128]{3,2,1,0:T(8,128)S(1)} %copy-done.1), custom_call_target="tpu_custom_call" | custom-call | flops 19327352832 | bytes 6291456 | tf_op jit(solution)/shard_map/pallas_call | solution.py:220
  53.0 0.2 reduce_sum.18
  53.4 0.6 broadcast_in_dim.43
  54.0 9.1 %all-to-all-start = ((f32[32,1,64]{2,1,0:T(1,128)}), f32[32,1,64]{2,1,0:T(1,128)S(1)}, u32[]{:S(2)}, u32[]{:S(2)}) async-start(f32[32,1,64]{2,1,0:T(1,128)} %broadcast_in_dim.43), calls=%async_computation | async-start | bytes 32768 | tf_op jit(solution)/shard_map/all_to_all | solution.py:371
  63.3 1.6 %collective-permute-start.1 = (f32[4,1,2,2,128]{4,3,2,1,0:T(2,128)S(1)}, f32[4,1,2,2,128]{4,3,2,1,0:T(2,128)S(1)}, u32[]{:S(2)}, u32[]{:S(2)}) collective-permute-start(f32[4,1,2,2,128]{4,3,2,1,0:T(2,128)S(1)} %get-tuple-element.15), channel_id=1, source_target_pairs={{8,0},{16,8},{24,16},{0,24},{9,1},{17,9},{25,17},{1,25},{10,2},{18... | collective-permute-start | bytes 24584 | tf_op jit(solution)/shard_map/ppermute | solution.py:33
  65.0 1.2 %collective-permute-done.1 = f32[4,1,2,2,128]{4,3,2,1,0:T(2,128)S(1)} collective-permute-done((f32[4,1,2,2,128]{4,3,2,1,0:T(2,128)S(1)}, f32[4,1,2,2,128]{4,3,2,1,0:T(2,128)S(1)}, u32[]{:S(2)}, u32[]{:S(2)}) %collective-permute-start.1) | collective-permute-done | bytes 8224 | tf_op jit(solution)/shard_map/ppermute | solution.py:33
  66.2 1.7 %collective-permute-done = f32[4,1,2,2,128]{4,3,2,1,0:T(2,128)S(1)} collective-permute-done((f32[4,1,2,2,128]{4,3,2,1,0:T(2,128)S(1)}, f32[4,1,2,2,128]{4,3,2,1,0:T(2,128)S(1)}, u32[]{:S(2)}, u32[]{:S(2)}) %collective-permute-start) | collective-permute-done | bytes 8224 | tf_op jit(solution)/shard_map/ppermute | solution.py:31
  68.0 3.4 %collective-permute-start.3 = (f32[4,4,1,2,128]{4,3,2,1,0:T(2,128)S(1)}, f32[4,4,1,2,128]{4,3,2,1,0:T(2,128)S(1)}, u32[]{:S(2)}, u32[]{:S(2)}) collective-permute-start(f32[4,4,1,2,128]{4,3,2,1,0:T(2,128)S(1)} %get-tuple-element.13), channel_id=1, source_target_pairs={{2,0},{4,2},{6,4},{0,6},{3,1},{5,3},{7,5},{1,7},{10,8},{12,10},{14... | collective-permute-start | bytes 49160 | tf_op jit(solution)/shard_map/ppermute | solution.py:33
  71.4 1.4 %collective-permute-done.3 = f32[4,4,1,2,128]{4,3,2,1,0:T(2,128)S(1)} collective-permute-done((f32[4,4,1,2,128]{4,3,2,1,0:T(2,128)S(1)}, f32[4,4,1,2,128]{4,3,2,1,0:T(2,128)S(1)}, u32[]{:S(2)}, u32[]{:S(2)}) %collective-permute-start.3) | collective-permute-done | bytes 16416 | tf_op jit(solution)/shard_map/ppermute | solution.py:33
  72.8 4.1 %collective-permute-done.2 = f32[4,4,1,2,128]{4,3,2,1,0:T(2,128)S(1)} collective-permute-done((f32[4,4,1,2,128]{4,3,2,1,0:T(2,128)S(1)}, f32[4,4,1,2,128]{4,3,2,1,0:T(2,128)S(1)}, u32[]{:S(2)}, u32[]{:S(2)}) %collective-permute-start.2) | collective-permute-done | bytes 16416 | tf_op jit(solution)/shard_map/ppermute | solution.py:31
  76.9 0.7 fusion.9
  77.6 1.5 %collective-permute-start.5 = (f32[4,4,4,1,128]{4,3,2,1,0:T(1,128)}, f32[4,4,4,1,128]{4,3,2,1,0:T(1,128)}, u32[]{:S(2)}, u32[]{:S(2)}) collective-permute-start(f32[4,4,4,1,128]{4,3,2,1,0:T(1,128)} %get-tuple-element.11), channel_id=1, source_target_pairs={{1,0},{0,1},{3,2},{2,3},{5,4},{4,5},{7,6},{6,7},{9,8},{8,9},{11,10... | collective-permute-start | bytes 98312 | tf_op jit(solution)/shard_map/ppermute | solution.py:33
  79.1 0.5 collective-permute-start.4
  79.6 0.5 broadcast.110
  80.1 0.7 reduce.4
  80.8 0.2 reshape.69.table_ref
  81.0 0.8 collective-permute-done.5
  81.8 1.5 %collective-permute-done.4 = f32[4,4,4,1,128]{4,3,2,1,0:T(1,128)} collective-permute-done((f32[4,4,4,1,128]{4,3,2,1,0:T(1,128)}, f32[4,4,4,1,128]{4,3,2,1,0:T(1,128)}, u32[]{:S(2)}, u32[]{:S(2)}) %collective-permute-start.4) | collective-permute-done | bytes 32800 | tf_op jit(solution)/shard_map/ppermute | solution.py:31
  83.3 0.9 pad_maximum_fusion
  84.3 13.0 %shard_map.105.pair_ref = f32[3,8,128]{2,1,0:T(8,128)S(1)} custom-call(f32[4,64,128]{2,1,0:T(8,128)S(1)} %pad_maximum_fusion.1.around_ref, f32[3,8,128]{2,1,0:T(8,128)S(1)} %pad_maximum_fusion.5.own_ref, f32[8,128]{1,0:T(8,128)S(1)} %bitcast.24), custom_call_target="tpu_custom_call" | custom-call | flops 53084160 | bytes 131072 | tf_op jit(solution)/shard_map/pallas_call | solution.py:375
  97.3 6.3 %shard_map.106 = f32[3,8,128]{2,1,0:T(8,128)} custom-call(s32[32,128]{1,0:T(8,128)S(1)} %bitcast_select_fusion.list_ref, f32[512,4]{1,0:T(8,128)S(1)} %reshape.69.table_ref, f32[3,8,128]{2,1,0:T(8,128)S(1)} %pad_maximum_fusion.4.coords_ref, f32[8,128]{1,0:T(8,128)S(1)} %bitcast.23, f32[3,8,128]{2,1,0:T(8,128)S(1)} %shard_map.105.pair_ref), custom_call_target="tpu_custom_call" | custom-call | tf_op jit(solution)/shard_map/pallas_call | solution.py:388
  103.7 1.7 %copy.20 = f32[16,3,128,128]{3,2,1,0:T(8,128)} copy(f32[16,3,128,128]{3,2,1,0:T(8,128)S(1)} %get-tuple-element.30) | data formatting | bytes 6291456
  (39 shorter events, 0.8 us)
Async XLA Ops:
  1.5 1.9 %copy-start.1 = (f32[16,3,128,128]{3,2,1,0:T(8,128)S(1)}, f32[16,3,128,128]{3,2,1,0:T(8,128)}, u32[]{:S(2)}) copy-start(f32[16,3,128,128]{3,2,1,0:T(8,128)} %density_ref.1) | copy-start | bytes 9437188
  3.4 49.8 %copy-start.5 = (f32[4,16]{1,0:T(4,128)S(1)}, f32[4,16]{1,0:T(4,128)}, u32[]{:S(2)}) copy-start(f32[4,16]{1,0:T(4,128)} %param.11) | copy-start | bytes 772
  3.4 59.8 %copy-start.4 = (s32[2,2,2,128]{3,2,1,0:T(2,128)S(1)}, s32[2,2,2,128]{3,2,1,0:T(2,128)}, u32[]{:S(2)}) copy-start(s32[2,2,2,128]{3,2,1,0:T(2,128)} %param.13) | copy-start | bytes 12292
  3.4 59.8 %copy-start.7 = (f32[8]{0:T(128)S(1)}, f32[8]{0:T(128)}, u32[]{:S(2)}) copy-start(f32[8]{0:T(128)} %param.15) | copy-start | bytes 100
  3.4 59.9 %copy-start.2 = (f32[3,2,2,2,128]{4,3,2,1,0:T(2,128)S(1)}, f32[3,2,2,2,128]{4,3,2,1,0:T(2,128)}, u32[]{:S(2)}) copy-start(f32[3,2,2,2,128]{4,3,2,1,0:T(2,128)} %param.12) | copy-start | bytes 36868
  3.4 61.5 %copy-start.3 = (s32[1,32,128]{2,1,0:T(8,128)S(1)}, s32[1,32,128]{2,1,0:T(8,128)}, u32[]{:S(2)}) copy-start(s32[1,32,128]{2,1,0:T(8,128)} %param.16) | copy-start | bytes 49156
  3.4 61.5 %copy-start.6 = (s32[1,32]{1,0:T(1,128)S(1)}, s32[1,32]{1,0:T(1,128)}, u32[]{:S(2)}) copy-start(s32[1,32]{1,0:T(1,128)} %param.17) | copy-start | bytes 388
  54.0 25.7 %all-to-all-start = ((f32[32,1,64]{2,1,0:T(1,128)}), f32[32,1,64]{2,1,0:T(1,128)S(1)}, u32[]{:S(2)}, u32[]{:S(2)}) async-start(f32[32,1,64]{2,1,0:T(1,128)} %broadcast_in_dim.43), calls=%async_computation | async-start | bytes 32768 | tf_op jit(solution)/shard_map/all_to_all | solution.py:371
  63.3 2.9 %collective-permute-start.1 = (f32[4,1,2,2,128]{4,3,2,1,0:T(2,128)S(1)}, f32[4,1,2,2,128]{4,3,2,1,0:T(2,128)S(1)}, u32[]{:S(2)}, u32[]{:S(2)}) collective-permute-start(f32[4,1,2,2,128]{4,3,2,1,0:T(2,128)S(1)} %get-tuple-element.15), channel_id=1, source_target_pairs={{8,0},{16,8},{24,16},{0,24},{9,1},{17,9},{25,17},{1,25},{10,2},{18... | collective-permute-start | bytes 24584 | tf_op jit(solution)/shard_map/ppermute | solution.py:33
  64.8 3.1 %collective-permute-start = (f32[4,1,2,2,128]{4,3,2,1,0:T(2,128)S(1)}, f32[4,1,2,2,128]{4,3,2,1,0:T(2,128)S(1)}, u32[]{:S(2)}, u32[]{:S(2)}) collective-permute-start(f32[4,1,2,2,128]{4,3,2,1,0:T(2,128)S(1)} %get-tuple-element.14), channel_id=1, source_target_pairs={{0,8},{8,16},{16,24},{24,0},{1,9},{9,17},{17,25},{25,1},{2,10},{10... | collective-permute-start | bytes 24584 | tf_op jit(solution)/shard_map/ppermute | solution.py:31
  68.0 4.8 %collective-permute-start.3 = (f32[4,4,1,2,128]{4,3,2,1,0:T(2,128)S(1)}, f32[4,4,1,2,128]{4,3,2,1,0:T(2,128)S(1)}, u32[]{:S(2)}, u32[]{:S(2)}) collective-permute-start(f32[4,4,1,2,128]{4,3,2,1,0:T(2,128)S(1)} %get-tuple-element.13), channel_id=1, source_target_pairs={{2,0},{4,2},{6,4},{0,6},{3,1},{5,3},{7,5},{1,7},{10,8},{12,10},{14... | collective-permute-start | bytes 49160 | tf_op jit(solution)/shard_map/ppermute | solution.py:33
  71.3 5.5 %collective-permute-start.2 = (f32[4,4,1,2,128]{4,3,2,1,0:T(2,128)S(1)}, f32[4,4,1,2,128]{4,3,2,1,0:T(2,128)S(1)}, u32[]{:S(2)}, u32[]{:S(2)}) collective-permute-start(f32[4,4,1,2,128]{4,3,2,1,0:T(2,128)S(1)} %get-tuple-element.12), channel_id=1, source_target_pairs={{0,2},{2,4},{4,6},{6,0},{1,3},{3,5},{5,7},{7,1},{8,10},{10,12},{12... | collective-permute-start | bytes 49160 | tf_op jit(solution)/shard_map/ppermute | solution.py:31
  77.6 4.2 %collective-permute-start.5 = (f32[4,4,4,1,128]{4,3,2,1,0:T(1,128)}, f32[4,4,4,1,128]{4,3,2,1,0:T(1,128)}, u32[]{:S(2)}, u32[]{:S(2)}) collective-permute-start(f32[4,4,4,1,128]{4,3,2,1,0:T(1,128)} %get-tuple-element.11), channel_id=1, source_target_pairs={{1,0},{0,1},{3,2},{2,3},{5,4},{4,5},{7,6},{6,7},{9,8},{8,9},{11,10... | collective-permute-start | bytes 98312 | tf_op jit(solution)/shard_map/ppermute | solution.py:33
  79.1 4.2 %collective-permute-start.4 = (f32[4,4,4,1,128]{4,3,2,1,0:T(1,128)}, f32[4,4,4,1,128]{4,3,2,1,0:T(1,128)}, u32[]{:S(2)}, u32[]{:S(2)}) collective-permute-start(f32[4,4,4,1,128]{4,3,2,1,0:T(1,128)} %get-tuple-element.10), channel_id=1, source_target_pairs={{0,1},{1,0},{2,3},{3,2},{4,5},{5,4},{6,7},{7,6},{8,9},{9,8},{10,11... | collective-permute-start | bytes 98312 | tf_op jit(solution)/shard_map/ppermute | solution.py:31
  84.3 13.0 %copy-start = (f32[2,2,2,128]{3,2,1,0:T(2,128)S(1)}, f32[2,2,2,128]{3,2,1,0:T(2,128)}, u32[]{:S(2)}) copy-start(f32[2,2,2,128]{3,2,1,0:T(2,128)} %param.14) | copy-start | bytes 12292

commit v4 on v3

--- a/solution.py
+++ b/solution.py
@@ -365,6 +365,7 @@
         ]
     ).reshape((3,) + flat)
 
+    keep_mask, around = lax.optimization_barrier((keep_mask, around))
     current, diagonal = purify(density, keep_mask, sizes)
     qm_charge = qm_sites[3] - jnp.mean(diagonal[:, 0], axis=1)
     table = jnp.concatenate([qm_sites[:3], qm_charge[None]], axis=0).T

time: 106 us -> 101 us (0.953)
  waiting for transfers between devices: 10.7 us -> 5.29 us
  Pallas kernels: 68.9 us -> 63.9 us
  other arithmetic: 2.28 us -> 6.48 us
  starting transfers between devices: 16.1 us -> 18.4 us
    pallas_call x1, Pallas kernels: 49.5 us -> 44.6 us  [purify(): pl.pallas_call(functools.partial(purify_kernel, sizes), out_shape=(jax.Sh...]
    ppermute x3, starting transfers between devices: 0.53 us -> 4.53 us  [padded(): lax.ppermute(tail, axis, [(i, (i + 1) % count) for i in range(count)])]
    ppermute x3, waiting for transfers between devices: 7.31 us -> 3.7 us  [padded(): lax.ppermute(tail, axis, [(i, (i + 1) % count) for i in range(count)])]
    ppermute x3, starting transfers between devices: 6.44 us -> 4.52 us  [padded(): lax.ppermute(head, axis, [((i + 1) % count, i) for i in range(count)])]
    ppermute x3, waiting for transfers between devices: 3.43 us -> 1.59 us  [padded(): lax.ppermute(head, axis, [((i + 1) % count, i) for i in range(count)])]
    concatenate x3, other arithmetic: 0.91 us -> 2.27 us  [padded(): jnp.concatenate([lax.ppermute(tail, axis, [(i, (i + 1) % count) for i in...]
    unnamed x18 -> x8, local copies, waits for them, and re-layouts: 4.35 us -> 4.32 us
  transfers between devices with their start and end apart: 7 -> 7, of which waited for: 6 -> 4; matrix products, arithmetic and copies ran while one was open for 2% -> 2% of each run, Pallas kernels for 0% -> 13%
where the time goes in v4:
time: 101 us
  Pallas kernels  63.9 us (63%)
  starting transfers between devices  18.4 us (18%)
  other arithmetic  6.48 us (6%)
  local copies, waits for them, and re-layouts  5.88 us (6%)
  waiting for transfers between devices  5.29 us (5%)
    pallas_call x1, Pallas kernels, purify(): pl.pallas_call(functools.partial(purify_kernel, sizes), out_shape=(jax.Sh...  44.6 us
    pallas_call x1, Pallas kernels, per_device(): pl.pallas_call(functools.partial(pair_kernel, cells), out_shape=jax.Shape...  13 us
    all_to_all x1, starting transfers between devices, per_device(): lax.all_to_all(jnp.broadcast_to(table.reshape(1, -1), (device_count, tabl...  9.32 us
    pallas_call x1, Pallas kernels, per_device(): pl.pallas_call(functools.partial(embed_kernel, row_count), out_shape=jax....  6.31 us
    ppermute x3, starting transfers between devices, padded(): lax.ppermute(tail, axis, [(i, (i + 1) % count) for i in range(count)])  4.53 us
    ppermute x3, starting transfers between devices, padded(): lax.ppermute(head, axis, [((i + 1) % count, i) for i in range(count)])  4.52 us
    unnamed x8, local copies, waits for them, and re-layouts  4.32 us
    ppermute x3, waiting for transfers between devices, padded(): lax.ppermute(tail, axis, [(i, (i + 1) % count) for i in range(count)])  3.7 us
  transfers between devices with their start and end apart: 7, of which 4 were waited for; matrix products, arithmetic and copies ran while one was open for 2% of the time, Pallas kernels for 13%

profile of v4, /device:TPU:0, one launch (start us, length us, event | category | flops | bytes accessed | tf_op | source)
XLA Modules:
  0.0 100.7 jit_solution(17596592250411065391)
XLA Ops:
  0.6 0.8 select_reduce_fusion
  1.4 0.7 fusion.3
  2.7 2.0 %collective-permute-start.1 = (f32[4,1,2,2,128]{4,3,2,1,0:T(2,128)S(1)}, f32[4,1,2,2,128]{4,3,2,1,0:T(2,128)S(1)}, u32[]{:S(2)}, u32[]{:S(2)}) collective-permute-start(f32[4,1,2,2,128]{4,3,2,1,0:T(2,128)S(1)} %get-tuple-element.19), channel_id=1, source_target_pairs={{8,0},{16,8},{24,16},{0,24},{9,1},{17,9},{25,17},{1,25},{10,2},{18... | collective-permute-start | bytes 24584 | tf_op jit(solution)/shard_map/ppermute | solution.py:33
  4.7 0.8 copy.17
  5.4 0.8 bitcast_select_fusion.list_ref
  6.2 0.8 add_multiply_fusion.2
  7.1 0.7 pad_maximum_fusion.3
  7.9 2.4 %collective-permute-start.2 = (f32[4,4,1,2,128]{4,3,2,1,0:T(2,128)S(1)}, f32[4,4,1,2,128]{4,3,2,1,0:T(2,128)S(1)}, u32[]{:S(2)}, u32[]{:S(2)}) collective-permute-start(f32[4,4,1,2,128]{4,3,2,1,0:T(2,128)S(1)} %get-tuple-element.16), channel_id=1, source_target_pairs={{0,2},{2,4},{4,6},{6,0},{1,3},{3,5},{5,7},{7,1},{8,10},{10,12},{12... | collective-permute-start | bytes 49160 | tf_op jit(solution)/shard_map/ppermute | solution.py:31
  10.2 2.1 %collective-permute-start.3 = (f32[4,4,1,2,128]{4,3,2,1,0:T(2,128)S(1)}, f32[4,4,1,2,128]{4,3,2,1,0:T(2,128)S(1)}, u32[]{:S(2)}, u32[]{:S(2)}) collective-permute-start(f32[4,4,1,2,128]{4,3,2,1,0:T(2,128)S(1)} %get-tuple-element.17), channel_id=1, source_target_pairs={{2,0},{4,2},{6,4},{0,6},{3,1},{5,3},{7,5},{1,7},{10,8},{12,10},{14... | collective-permute-start | bytes 49160 | tf_op jit(solution)/shard_map/ppermute | solution.py:33
  12.3 1.8 %collective-permute-done.2 = f32[4,4,1,2,128]{4,3,2,1,0:T(2,128)S(1)} collective-permute-done((f32[4,4,1,2,128]{4,3,2,1,0:T(2,128)S(1)}, f32[4,4,1,2,128]{4,3,2,1,0:T(2,128)S(1)}, u32[]{:S(2)}, u32[]{:S(2)}) %collective-permute-start.2) | collective-permute-done | bytes 16416 | tf_op jit(solution)/shard_map/ppermute | solution.py:31
  14.2 0.7 pad_maximum_fusion.2
  15.0 1.7 %collective-permute-start.4 = (f32[4,4,4,1,128]{4,3,2,1,0:T(1,128)S(1)}, f32[4,4,4,1,128]{4,3,2,1,0:T(1,128)S(1)}, u32[]{:S(2)}, u32[]{:S(2)}) collective-permute-start(f32[4,4,4,1,128]{4,3,2,1,0:T(1,128)S(1)} %get-tuple-element.14), channel_id=1, source_target_pairs={{0,1},{1,0},{2,3},{3,2},{4,5},{5,4},{6,7},{7,6},{8,9},{9,8},{10,11... | collective-permute-start | bytes 98312 | tf_op jit(solution)/shard_map/ppermute | solution.py:31
  17.1 1.9 %collective-permute-done.4 = f32[4,4,4,1,128]{4,3,2,1,0:T(1,128)S(1)} collective-permute-done((f32[4,4,4,1,128]{4,3,2,1,0:T(1,128)S(1)}, f32[4,4,4,1,128]{4,3,2,1,0:T(1,128)S(1)}, u32[]{:S(2)}, u32[]{:S(2)}) %collective-permute-start.4) | collective-permute-done | bytes 32800 | tf_op jit(solution)/shard_map/ppermute | solution.py:31
  19.0 1.5 %collective-permute-done.5 = f32[4,4,4,1,128]{4,3,2,1,0:T(1,128)S(1)} collective-permute-done((f32[4,4,4,1,128]{4,3,2,1,0:T(1,128)S(1)}, f32[4,4,4,1,128]{4,3,2,1,0:T(1,128)S(1)}, u32[]{:S(2)}, u32[]{:S(2)}) %collective-permute-start.5) | collective-permute-done | bytes 32800 | tf_op jit(solution)/shard_map/ppermute | solution.py:33
  20.5 0.8 pad_maximum_fusion
  21.5 1.9 %copy-done.1 = f32[16,3,128,128]{3,2,1,0:T(8,128)S(1)} copy-done((f32[16,3,128,128]{3,2,1,0:T(8,128)S(1)}, f32[16,3,128,128]{3,2,1,0:T(8,128)}, u32[]{:S(2)}) %copy-start.1) | copy-done | bytes 3145752
  23.3 44.6 %shard_map.104 = (f32[16,3,128,128]{3,2,1,0:T(8,128)S(1)}, f32[16,1,128]{2,1,0:T(1,128)S(1)}) custom-call(f32[16,3]{1,0:T(8,128)S(1)} %fusion.8.keep_ref, f32[16,3,128,128]{3,2,1,0:T(8,128)S(1)} %copy-done.1), custom_call_target="tpu_custom_call" | custom-call | flops 19327352832 | bytes 6291456 | tf_op jit(solution)/shard_map/pallas_call | solution.py:220
  68.3 0.6 broadcast_in_dim.45
  69.0 9.3 %all-to-all-start = ((f32[32,1,64]{2,1,0:T(1,128)}), f32[32,1,64]{2,1,0:T(1,128)S(1)}, u32[]{:S(2)}, u32[]{:S(2)}) async-start(f32[32,1,64]{2,1,0:T(1,128)} %broadcast_in_dim.45), calls=%async_computation | async-start | bytes 32768 | tf_op jit(solution)/shard_map/all_to_all | solution.py:372
  78.3 13.0 %shard_map.105.pair_ref = f32[3,8,128]{2,1,0:T(8,128)S(1)} custom-call(f32[4,64,128]{2,1,0:T(8,128)S(1)} %pad_maximum_fusion.1.around_ref, f32[3,8,128]{2,1,0:T(8,128)S(1)} %pad_maximum_fusion.5.own_ref, f32[8,128]{1,0:T(8,128)S(1)} %bitcast.24), custom_call_target="tpu_custom_call" | custom-call | flops 53084160 | bytes 131072 | tf_op jit(solution)/shard_map/pallas_call | solution.py:376
  91.3 0.5 broadcast.110
  91.9 0.7 reduce.4
  92.7 6.3 %shard_map.106 = f32[3,8,128]{2,1,0:T(8,128)} custom-call(s32[32,128]{1,0:T(8,128)S(1)} %bitcast_select_fusion.list_ref, f32[512,4]{1,0:T(8,128)S(1)} %reshape.69.table_ref, f32[3,8,128]{2,1,0:T(8,128)S(1)} %pad_maximum_fusion.4.coords_ref, f32[8,128]{1,0:T(8,128)S(1)} %bitcast.23, f32[3,8,128]{2,1,0:T(8,128)S(1)} %shard_map.105.pair_ref), custom_call_target="tpu_custom_call" | custom-call | tf_op jit(solution)/shard_map/pallas_call | solution.py:389
  99.0 1.7 %copy.20 = f32[16,3,128,128]{3,2,1,0:T(8,128)} copy(f32[16,3,128,128]{3,2,1,0:T(8,128)S(1)} %get-tuple-element.34) | data formatting | bytes 6291456
  (29 shorter events, 1.8 us)
Async XLA Ops:
  2.2 4.9 %collective-permute-start = (f32[4,1,2,2,128]{4,3,2,1,0:T(2,128)S(1)}, f32[4,1,2,2,128]{4,3,2,1,0:T(2,128)S(1)}, u32[]{:S(2)}, u32[]{:S(2)}) collective-permute-start(f32[4,1,2,2,128]{4,3,2,1,0:T(2,128)S(1)} %get-tuple-element.18), channel_id=1, source_target_pairs={{0,8},{8,16},{16,24},{24,0},{1,9},{9,17},{17,25},{25,1},{2,10},{10... | collective-permute-start | bytes 24584 | tf_op jit(solution)/shard_map/ppermute | solution.py:31
  2.7 4.4 %collective-permute-start.1 = (f32[4,1,2,2,128]{4,3,2,1,0:T(2,128)S(1)}, f32[4,1,2,2,128]{4,3,2,1,0:T(2,128)S(1)}, u32[]{:S(2)}, u32[]{:S(2)}) collective-permute-start(f32[4,1,2,2,128]{4,3,2,1,0:T(2,128)S(1)} %get-tuple-element.19), channel_id=1, source_target_pairs={{8,0},{16,8},{24,16},{0,24},{9,1},{17,9},{25,17},{1,25},{10,2},{18... | collective-permute-start | bytes 24584 | tf_op jit(solution)/shard_map/ppermute | solution.py:33
  7.9 6.2 %collective-permute-start.2 = (f32[4,4,1,2,128]{4,3,2,1,0:T(2,128)S(1)}, f32[4,4,1,2,128]{4,3,2,1,0:T(2,128)S(1)}, u32[]{:S(2)}, u32[]{:S(2)}) collective-permute-start(f32[4,4,1,2,128]{4,3,2,1,0:T(2,128)S(1)} %get-tuple-element.16), channel_id=1, source_target_pairs={{0,2},{2,4},{4,6},{6,0},{1,3},{3,5},{5,7},{7,1},{8,10},{10,12},{12... | collective-permute-start | bytes 49160 | tf_op jit(solution)/shard_map/ppermute | solution.py:31
  10.2 3.9 %collective-permute-start.3 = (f32[4,4,1,2,128]{4,3,2,1,0:T(2,128)S(1)}, f32[4,4,1,2,128]{4,3,2,1,0:T(2,128)S(1)}, u32[]{:S(2)}, u32[]{:S(2)}) collective-permute-start(f32[4,4,1,2,128]{4,3,2,1,0:T(2,128)S(1)} %get-tuple-element.17), channel_id=1, source_target_pairs={{2,0},{4,2},{6,4},{0,6},{3,1},{5,3},{7,5},{1,7},{10,8},{12,10},{14... | collective-permute-start | bytes 49160 | tf_op jit(solution)/shard_map/ppermute | solution.py:33
  15.0 4.0 %collective-permute-start.4 = (f32[4,4,4,1,128]{4,3,2,1,0:T(1,128)S(1)}, f32[4,4,4,1,128]{4,3,2,1,0:T(1,128)S(1)}, u32[]{:S(2)}, u32[]{:S(2)}) collective-permute-start(f32[4,4,4,1,128]{4,3,2,1,0:T(1,128)S(1)} %get-tuple-element.14), channel_id=1, source_target_pairs={{0,1},{1,0},{2,3},{3,2},{4,5},{5,4},{6,7},{7,6},{8,9},{9,8},{10,11... | collective-permute-start | bytes 98312 | tf_op jit(solution)/shard_map/ppermute | solution.py:31
  16.6 3.9 %collective-permute-start.5 = (f32[4,4,4,1,128]{4,3,2,1,0:T(1,128)S(1)}, f32[4,4,4,1,128]{4,3,2,1,0:T(1,128)S(1)}, u32[]{:S(2)}, u32[]{:S(2)}) collective-permute-start(f32[4,4,4,1,128]{4,3,2,1,0:T(1,128)S(1)} %get-tuple-element.15), channel_id=1, source_target_pairs={{1,0},{0,1},{3,2},{2,3},{5,4},{4,5},{7,6},{6,7},{9,8},{8,9},{11,10... | collective-permute-start | bytes 98312 | tf_op jit(solution)/shard_map/ppermute | solution.py:33
  21.5 1.9 %copy-start.1 = (f32[16,3,128,128]{3,2,1,0:T(8,128)S(1)}, f32[16,3,128,128]{3,2,1,0:T(8,128)}, u32[]{:S(2)}) copy-start(f32[16,3,128,128]{3,2,1,0:T(8,128)} %density_ref.1) | copy-start | bytes 9437188
  23.3 44.8 %copy-start.2 = (f32[4,16]{1,0:T(4,128)S(1)}, f32[4,16]{1,0:T(4,128)}, u32[]{:S(2)}) copy-start(f32[4,16]{1,0:T(4,128)} %param.11) | copy-start | bytes 772
  69.0 22.3 %all-to-all-start = ((f32[32,1,64]{2,1,0:T(1,128)}), f32[32,1,64]{2,1,0:T(1,128)S(1)}, u32[]{:S(2)}, u32[]{:S(2)}) async-start(f32[32,1,64]{2,1,0:T(1,128)} %broadcast_in_dim.45), calls=%async_computation | async-start | bytes 32768 | tf_op jit(solution)/shard_map/all_to_all | solution.py:372
  78.3 14.4 %copy-start = (f32[2,2,2,128]{3,2,1,0:T(2,128)S(1)}, f32[2,2,2,128]{3,2,1,0:T(2,128)}, u32[]{:S(2)}) copy-start(f32[2,2,2,128]{3,2,1,0:T(2,128)} %param.14) | copy-start | bytes 12292
